TPU v7x, 256 devices: a whole 4x4x8 slice. The times are simulated.
256 devices in a mesh: group: 16 (over y, x), dev: 16 (over z, core).
Axes of the slice: x: 4, y: 4, z: 8, core: 2. Of those that a mesh axis runs over, the one named last changes fastest.
Arguments:
- points: float32 [3, 524288], P(None, ('group', 'dev')), may hold values from 0 to 1
- values: float32 [16, 524288], P(None, ('group', 'dev')), may hold values from -6 to 6
- counts: int32 [8192], P(('group', 'dev')), may hold values from 8 to 64, as said below
- leaf_basis: float32 [64, 524288], P(None, ('group', 'dev')), may hold values from -1 to 2
- local_pair: float32 [7936, 64, 128], P(('group', 'dev')), may hold values from -1 to 1
- chain_pair: float32 [256, 8, 64, 128], P(('group', 'dev')), may hold values from -1 to 1, as said below
- near_leaf: int32 [8192, 12], P(('group', 'dev')), may hold values from 0 to 31
- far_peer: int32 [8192, 4], P(('group', 'dev')), may hold values from 0 to 15, all different within a row; in each aligned block of 32 rows (0 to 31, 32 to 63, ...) at most 16 rows name the same one
- far_leaf: int32 [8192, 4], P(('group', 'dev')), may hold values from 0 to 31
- leaf_coupling: bfloat16 [4, 64, 524288], P(None, None, ('group', 'dev')), may hold values from -0.375 to 0.375
- group_far: int32 [16, 2], P('group'), may hold values from 0 to 14, all different within a row
- group_coupling: bfloat16 [2, 64, 1024], P(None, None, 'group'), may hold values from -0.75 to 0.75
Outputs:
- leaf_q: float32 [64, 524288], P(None, ('group', 'dev'))
- local_new: float32 [7936, 64, 128], P(('group', 'dev'))
- chain_new: float32 [256, 8, 64, 128], P(('group', 'dev'))
- product: float32 [16, 524288], P(None, ('group', 'dev'))
Inputs may be any that keep to these rules, and one draw needn't show every extreme that they name: `counts`: the first leaf of every block has 64 live points, the second 64 // 8. chain_pair[s, j] is the same for all blocks s with the same s >> (j + 1). `far_peer`: the 4 offsets of one leaf differ; among the leaves of one block no offset appears more than 16 times, and some block of every draw has an offset that appears exactly 16 times. `group_far`: the 2 offsets of one subtree root differ.
All inputs are finite; a program needn't handle non-finite values.
Results may differ from a plain program's by a relative error of at most 0.0003.
Values sent between devices are 32-bit elements; how exact they have to be, the bound alone decides.
No kernel may reach another device: no remote copies, remote signals or barrier semaphores. Data moves between devices by JAX's collectives and lax.ppermute only.
A program may use at most 128 MiB of HBM per device.

v0:
```python
import jax
import jax.numpy as jnp
from jax import lax
from jax.sharding import PartitionSpec as P

highest = lax.Precision.HIGHEST
soft_square = 0.01


def swapped(x, axis, distance):
    return lax.ppermute(x, axis, [(i, i ^ 1 << distance) for i in range(lax.axis_size(axis))])


def factor(stacked):
    gram_matrix = jnp.einsum("nam,nbm->nab", stacked, stacked, precision=highest)
    lowers = jnp.linalg.cholesky(gram_matrix)
    identity = jnp.broadcast_to(
        jnp.eye(gram_matrix.shape[-1], dtype=jnp.float32), gram_matrix.shape
    )
    inverse = jax.scipy.linalg.solve_triangular(lowers, identity, lower=True)
    return (jnp.einsum("nab,nbm->nam", inverse, stacked, precision=highest), lowers)


def combine(left_lower, right_lower, pair_rows):
    rank_size = left_lower.shape[-1]
    stacked = jnp.concatenate(
        [
            jnp.einsum("nab,nbc->nac", pair_rows[:, :, :rank_size], left_lower, precision=highest),
            jnp.einsum("nab,nbc->nac", pair_rows[:, :, rank_size:], right_lower, precision=highest),
        ],
        axis=2,
    )
    return factor(stacked)


def local_tree(stacked, pair_rows):
    leaf_count = stacked.shape[0]
    rank_size = stacked.shape[1]
    tree_depth = leaf_count.bit_length() - 1
    leaf_q, lowers = factor(stacked)
    new_levels = []
    for level_index in range(tree_depth - 1, -1, -1):
        parents = 2**level_index
        children = lowers.reshape(parents, 2, rank_size, rank_size)
        cluster_basis, lowers = combine(
            children[:, 0], children[:, 1], pair_rows[parents - 1 : 2 * parents - 1]
        )
        new_levels.insert(0, cluster_basis)
    return (leaf_q, jnp.concatenate(new_levels, axis=0), lowers[0])


def climb_local(coeffs, new_pairs):
    tree_depth = (new_pairs.shape[0] + 1).bit_length() - 1
    vectors, rank_size = (coeffs.shape[1], coeffs.shape[2])
    for level_index in range(tree_depth - 1, -1, -1):
        parents = 2**level_index
        joined = (
            coeffs.reshape(parents, 2, vectors, rank_size)
            .transpose(0, 2, 1, 3)
            .reshape(parents, vectors, 2 * rank_size)
        )
        coeffs = jnp.einsum(
            "nab,nvb->nva", new_pairs[parents - 1 : 2 * parents - 1], joined, precision=highest
        )
    return coeffs[0]


def descend_local(top_coeffs, new_pairs):
    tree_depth = (new_pairs.shape[0] + 1).bit_length() - 1
    vectors, rank_size = top_coeffs.shape
    coeffs = top_coeffs[None]
    for level_index in range(tree_depth):
        parents = 2**level_index
        spread = jnp.einsum(
            "nva,nab->nvb", coeffs, new_pairs[parents - 1 : 2 * parents - 1], precision=highest
        )
        coeffs = (
            spread.reshape(parents, vectors, 2, rank_size)
            .transpose(0, 2, 1, 3)
            .reshape(2 * parents, vectors, rank_size)
        )
    return coeffs


def near_field(coords, near_rows, masked, near_scale):
    near_coords = coords[:, near_rows]
    leaf_count, near_count, rank_size = (
        near_coords.shape[1],
        near_coords.shape[2],
        near_coords.shape[3],
    )
    square = jnp.zeros((leaf_count, near_count, rank_size, rank_size), jnp.float32)
    for axis_index in range(3):
        gap_value = coords[axis_index][:, None, :, None] - near_coords[axis_index][:, :, None, :]
        square = square + gap_value * gap_value
    kernel = 1.0 / jnp.sqrt(square + soft_square)
    return near_scale * jnp.einsum("pnxq,pnvq->pvx", kernel, masked[near_rows], precision=highest)


def half_block(chain_q, which_side):
    rank_size = chain_q.shape[0]
    return jnp.where(which_side == 1, chain_q[:, rank_size:], chain_q[:, :rank_size])


def per_device(
    points,
    values,
    counts,
    leaf_basis,
    local_pair,
    chain_pair,
    near_leaf,
    far_peer,
    far_leaf,
    leaf_coupling,
    group_far,
    group_coupling,
):
    rank_size = leaf_basis.shape[0]
    leaf_count = counts.shape[0]
    vectors = values.shape[0]
    far_slots = far_peer.shape[1]
    dev_width = lax.axis_size("dev")
    group_width = lax.axis_size("group")
    dev_levels = dev_width.bit_length() - 1
    group_levels = group_width.bit_length() - 1
    dev_index = lax.axis_index("dev")
    group_index = lax.axis_index("group")
    stacked = leaf_basis.reshape(rank_size, leaf_count, rank_size).transpose(1, 0, 2)
    leaf_q, new_pairs, root_lower = local_tree(stacked, local_pair)
    live_mask = (
        lax.broadcasted_iota(jnp.int32, (leaf_count, rank_size), 1) < counts[:, None]
    ).astype(jnp.float32)
    masked = (
        values.reshape(vectors, leaf_count, rank_size).transpose(1, 0, 2) * live_mask[:, None, :]
    )
    coeffs = jnp.einsum("pax,pvx->pva", leaf_q, masked, precision=highest)
    root_coeffs = climb_local(coeffs, new_pairs)
    chain_bases = []
    current = root_lower
    for level_index in range(dev_levels + group_levels):
        if level_index < dev_levels:
            which_side = dev_index >> level_index & 1
            partner = swapped(current, "dev", level_index)
        else:
            which_side = group_index >> level_index - dev_levels & 1
            partner = swapped(current, "group", level_index - dev_levels)
        left_lower = jnp.where(which_side == 0, current, partner)
        right_lower = jnp.where(which_side == 0, partner, current)
        cluster_basis, lowers = combine(
            left_lower[None], right_lower[None], chain_pair[:, level_index]
        )
        current = lowers[0]
        chain_bases.append(cluster_basis[0])
    moving = root_coeffs
    for level_index in range(dev_levels):
        half_rows = half_block(chain_bases[level_index], dev_index >> level_index & 1)
        moving = jnp.einsum("ab,vb->va", half_rows, moving, precision=highest)
    group_total = lax.psum(moving, "dev")
    all_groups = lax.all_gather(group_total[None], "group", axis=0, tiled=True)
    source_groups = (group_index + 1 + group_far[0]) % group_width
    coupling = group_coupling.astype(jnp.float32)
    downward = jnp.einsum("fji,fvj->vi", coupling, all_groups[source_groups], precision=highest)
    for level_index in range(dev_levels - 1, -1, -1):
        half_rows = half_block(chain_bases[level_index], dev_index >> level_index & 1)
        downward = jnp.einsum("ab,va->vb", half_rows, downward, precision=highest)
    leaf_coeffs = descend_local(downward, new_pairs)
    coeff_rows = coeffs.reshape(leaf_count, vectors * rank_size)
    peer_dev = ((dev_index + far_peer) % dev_width).reshape(-1)
    capacity = min(leaf_count, 2 * leaf_count * far_slots // dev_width)
    onehot = (peer_dev[:, None] == jnp.arange(dev_width, dtype=jnp.int32)[None, :]).astype(
        jnp.int32
    )
    position = jnp.sum((jnp.cumsum(onehot, axis=0) - onehot) * onehot, axis=1)
    slot_index = peer_dev * capacity + position
    request = jnp.zeros((dev_width * capacity,), jnp.int32).at[slot_index].set(far_leaf.reshape(-1))
    replies = lax.all_to_all(
        jnp.take(
            coeff_rows,
            lax.all_to_all(
                request.reshape(dev_width, capacity), "dev", split_axis=0, concat_axis=0, tiled=True
            ),
            axis=0,
        ),
        "dev",
        split_axis=0,
        concat_axis=0,
        tiled=True,
    )
    sources = replies.reshape(dev_width * capacity, vectors * rank_size)[slot_index]
    sources = sources.reshape(leaf_count, far_slots, vectors, rank_size)
    leaf_far = jnp.einsum(
        "fjpi,pfvj->pvi",
        leaf_coupling.astype(jnp.float32).reshape(far_slots, rank_size, leaf_count, rank_size),
        sources,
        precision=highest,
    )
    far_field = jnp.einsum("pax,pva->pvx", leaf_q, leaf_coeffs + leaf_far, precision=highest)
    near_scale = float(rank_size * near_leaf.shape[1]) ** (-0.5)
    close_field = near_field(
        points.reshape(3, leaf_count, rank_size), near_leaf, masked, near_scale
    )
    product = (
        ((far_field + close_field) * live_mask[:, None, :])
        .transpose(1, 0, 2)
        .reshape(vectors, leaf_count * rank_size)
    )
    leaf_out = leaf_q.transpose(1, 0, 2).reshape(rank_size, leaf_count * rank_size)
    chain_out = jnp.stack(chain_bases, axis=0)[None]
    return (leaf_out, new_pairs, chain_out, product)


def solution(mesh):
    in_specs = (
        P(None, ("group", "dev")),
        P(None, ("group", "dev")),
        P(("group", "dev")),
        P(None, ("group", "dev")),
        P(("group", "dev"), None, None),
        P(("group", "dev"), None, None, None),
        P(("group", "dev"), None),
        P(("group", "dev"), None),
        P(("group", "dev"), None),
        P(None, None, ("group", "dev")),
        P("group", None),
        P(None, None, "group"),
    )
    out_specs = (
        P(None, ("group", "dev")),
        P(("group", "dev"), None, None),
        P(("group", "dev"), None, None, None),
        P(None, ("group", "dev")),
    )
    return jax.shard_map(
        per_device, mesh=mesh, in_specs=in_specs, out_specs=out_specs, check_vma=False
    )
```

profile of v0, /device:TPU:4, one launch (start us, length us, event | category | flops | bytes accessed | tf_op | source)
XLA Modules:
  0.0 910.8 jit_solution(12271723945596953663)
XLA Ops:
  0.7 1.5 reshape.597
  2.2 3.0 fusion.41
  6.6 188.4 %custom-call.46 = f32[32,64,64]{2,1,0:T(8,128)S(1)} custom-call(f32[32,64,64]{2,1,0:T(8,128)} %fusion.38), custom_call_target="Cholesky" | custom-call | tf_op jit(solution)/shard_map/jit(cholesky)/cholesky | solution.py:16
  196.4 2.9 select_bitcast_fusion
  199.3 2.6 copy.226
  205.5 94.5 %custom-call.48 = f32[16,64,64]{2,1,0:T(8,128)S(1)} custom-call(f32[16,64,64]{2,1,0:T(8,128)} %fusion.47), custom_call_target="Cholesky" | custom-call | tf_op jit(solution)/shard_map/jit(cholesky)/cholesky | solution.py:16
  303.4 47.6 %custom-call.49 = f32[8,64,64]{2,1,0:T(8,128)S(1)} custom-call(f32[8,64,64]{2,1,0:T(8,128)} %fusion.54), custom_call_target="Cholesky" | custom-call | tf_op jit(solution)/shard_map/jit(cholesky)/cholesky | solution.py:16
  354.1 24.2 %custom-call.50 = f32[4,64,64]{2,1,0:T(8,128)S(1)} custom-call(f32[4,64,64]{2,1,0:T(8,128)} %fusion.63), custom_call_target="Cholesky" | custom-call | tf_op jit(solution)/shard_map/jit(cholesky)/cholesky | solution.py:16
  379.5 12.1 %custom-call.51 = f32[2,64,64]{2,1,0:T(8,128)S(1)} custom-call(f32[2,64,64]{2,1,0:T(8,128)S(1)} %fusion.71), custom_call_target="Cholesky" | custom-call | tf_op jit(solution)/shard_map/jit(cholesky)/cholesky | solution.py:16
  392.6 5.8 custom-call.72
  399.2 1.3 fusion.154
  403.2 8.7 all-to-all-start
  412.5 4.9 custom-call.73
  418.5 9.8 %custom-call.52 = f32[2,1,64,64]{2,3,1,0:T(8,128)S(1)} custom-call(f32[2,1,64,64]{3,2,1,0:T(8,128)S(1)} %get-tuple-element.32), custom_call_target="InvertDiagBlocksLowerTriangular" | custom-call | tf_op jit(solution)/shard_map/jit(_solve_triangular)/vmap()/triangular_solve | solution.py:20
  428.3 19.7 %custom-call.53 = f32[4,1,64,64]{2,3,1,0:T(8,128)S(1)} custom-call(f32[4,1,64,64]{3,2,1,0:T(8,128)S(1)} %get-tuple-element.15), custom_call_target="InvertDiagBlocksLowerTriangular" | custom-call | tf_op jit(solution)/shard_map/jit(_solve_triangular)/vmap()/triangular_solve | solution.py:20
  450.0 39.3 %custom-call.54 = f32[8,1,64,64]{2,3,1,0:T(8,128)S(1)} custom-call(f32[8,1,64,64]{3,2,1,0:T(8,128)S(1)} %get-tuple-element.13), custom_call_target="InvertDiagBlocksLowerTriangular" | custom-call | tf_op jit(solution)/shard_map/jit(_solve_triangular)/vmap()/triangular_solve | solution.py:20
  489.3 1.3 fusion.52
  490.6 78.6 %custom-call.55 = f32[16,1,64,64]{2,3,1,0:T(8,128)S(1)} custom-call(f32[16,1,64,64]{3,2,1,0:T(8,128)S(1)} %get-tuple-element.11), custom_call_target="InvertDiagBlocksLowerTriangular" | custom-call | tf_op jit(solution)/shard_map/jit(_solve_triangular)/vmap()/triangular_solve | solution.py:20
  569.2 1.8 fusion.45
  571.0 68.6 %custom-call.47 = f32[32,1,64,64]{0,2,3,1:T(8,128)} custom-call(f32[32,1,64,64]{0,3,2,1:T(8,128)} %get-tuple-element.17), custom_call_target="InvertDiagBlocksLowerTriangular" | custom-call | tf_op jit(solution)/shard_map/jit(_solve_triangular)/vmap()/triangular_solve | solution.py:20
  639.6 2.9 copy.224
  643.6 1.7 fusion.39
  645.7 1.7 fusion.239
  648.3 1.8 reshape.644
  650.1 1.8 constant_dynamic-update-slice_fusion.3
  651.9 2.0 constant_dynamic-update-slice_fusion.2
  653.9 2.1 constant_dynamic-update-slice_fusion.1
  656.0 2.6 constant_dynamic-update-slice_fusion
  662.1 1.6 slice_bitcast_fusion.55
  669.3 4.4 reshape.662
  680.6 7.2 all-to-all-start.1
  687.8 2.8 gather_fusion.3
  690.6 2.4 gather_fusion.4
  693.2 1.7 copy-done.6
  694.9 15.4 %fusion.26 = f32[32,16,64]{2,1,0:T(8,128)} fusion(f32[32,12,16,64]{3,2,1,0:T(8,128)S(1)} %bitcast.596, f32[32,12,64]{2,1,0:T(8,128)S(1)} %get-tuple-element.21, f32[32,64]{1,0:T(8,128)S(1)} %copy-done.35, f32[32,12,64]{2,1,0:T(8,128)S(1)} %get-tuple-element.20, f32[32,64]{1,0:T(8,128)S(1)} %copy-done.34, f32[32,12,64]{2,1,0:T(8,128)S(1)} %get-tuple-element.19, ...), kind=kOutput, calls=%fused_computation.35 | convolution fusion | flops 316178432 | bytes 2023424 | tf_op jit(solution)/shard_map/pnxq,pnvq->pvx/dot_general | solution.py:97
  712.7 5.8 custom-call.74
  719.9 4.9 custom-call.75
  725.9 1.9 collective-permute-start.1
  728.1 1.8 collective-permute-done.1
  730.6 5.8 custom-call.76
  737.8 4.9 custom-call.77
  743.0 2.9 collective-permute-start.2
  748.7 5.8 custom-call.78
  756.0 4.9 custom-call.79
  761.1 6.5 collective-permute-start.3
  768.4 1.5 fusion.199
  770.8 5.8 custom-call.80
  778.0 4.9 custom-call.81
  784.9 24.1 %psum.7 = f32[1,16,64]{2,1,0:T(8,128)S(1)} all-reduce(f32[1,16,64]{2,1,0:T(8,128)S(1)} %convolution_bitcast_fusion.34), channel_id=1, replica_groups=mesh['group'=16,'dev'=16] {'dev'}, use_global_device_ids=true, to_apply=%region_12.15 | all-reduce | flops 1024 | bytes 8192 | tf_op jit(solution)/shard_map/psum | solution.py:159
  809.0 25.1 %all_gather.3 = f32[16,16,64]{2,1,0:T(8,128)} all-gather(f32[1,16,64]{2,1,0:T(8,128)S(1)} %psum.7), channel_id=1, replica_groups=mesh['group'=16,'dev'=16] {'group'}, dimensions={0}, use_global_device_ids=true | all-gather | bytes 69632 | tf_op jit(solution)/shard_map/all_gather | solution.py:160
  834.1 1.6 gather_fusion
  838.7 1.5 collective-permute-start.4
  840.3 2.5 collective-permute-done.4
  843.5 5.8 custom-call.82
  850.7 1.2 collective-permute-start.5
  851.9 4.9 custom-call.83
  858.7 5.8 custom-call.84
  867.1 4.9 custom-call.85
  873.9 5.8 custom-call.86
  881.1 3.0 collective-permute-start.7
  884.1 4.9 custom-call.87
  890.9 5.8 custom-call.88
  898.1 4.9 custom-call.89
  905.3 3.3 fusion.31
  (299 shorter events, 76.9 us)
Async XLA Ops:
  0.6 835.0 %copy-start = (bf16[2,64,64]{2,1,0:T(8,128)(2,1)S(1)}, bf16[2,64,64]{2,1,0:T(8,128)(2,1)}, u32[]{:S(2)}) copy-start(bf16[2,64,64]{2,1,0:T(8,128)(2,1)} %param.26) | copy-start | bytes 49156
  2.1 4.5 copy-start.1
  199.3 2.6 copy-start.5
  300.7 77.8 %copy-start.7 = (f32[8,64,64]{2,1,0:T(8,128)}, f32[8,64,64]{2,1,0:T(8,128)S(1)}, u32[]{:S(2)}) copy-start(f32[8,64,64]{2,1,0:T(8,128)S(1)} %convolution_bitcast_fusion.2) | copy-start | bytes 393220
  301.1 0.7 copy-start.9
  302.7 97.8 %copy-start.37 = (s32[32,4]{0,1:T(4,128)S(1)}, s32[32,4]{0,1:T(4,128)}, u32[]{:S(2)}) copy-start(s32[32,4]{0,1:T(4,128)} %param.22) | copy-start | bytes 1540
  302.7 98.6 %copy-start.36 = (s32[32,4]{0,1:T(4,128)S(1)}, s32[32,4]{0,1:T(4,128)}, u32[]{:S(2)}) copy-start(s32[32,4]{0,1:T(4,128)} %param.23) | copy-start | bytes 1540
  351.6 0.7 copy-start.13
  352.3 0.7 copy-start.15
  379.1 24.1 %copy-start.18 = (f32[2,64,64]{2,1,0:T(8,128)}, f32[2,64,64]{2,1,0:T(8,128)S(1)}, u32[]{:S(2)}) copy-start(f32[2,64,64]{2,1,0:T(8,128)S(1)} %convolution_bitcast_fusion.7) | copy-start | bytes 98308
  400.4 309.9 %collective-permute-start = (f32[64,64]{1,0:T(8,128)}, f32[64,64]{1,0:T(8,128)}, u32[]{:S(2)}, u32[]{:S(2)}) collective-permute-start(f32[64,64]{1,0:T(8,128)} %get-tuple-element.52), channel_id=1, source_target_pairs={{0,1},{1,0},{2,3},{3,2},{4,5},{5,4},{6,7},{7,6},{8,9},{9,8},{10,11... | collective-permute-start | bytes 49160 | tf_op jit(solution)/shard_map/ppermute | solution.py:11
  403.2 273.7 %all-to-all-start = ((s32[16,1,16]{2,1,0:T(1,128)}), s32[16,1,16]{2,1,0:T(1,128)}, u32[]{:S(2)}, u32[]{:S(2)}) async-start(s32[16,1,16]{2,1,0:T(1,128)} %all_to_all.13), calls=%async_computation | async-start | bytes 16384 | tf_op jit(solution)/shard_map/all_to_all | solution.py:180
  569.2 74.4 %copy-start.2 = (f32[64,32,64]{2,1,0:T(8,128)S(1)}, f32[64,32,64]{2,1,0:T(8,128)}, u32[]{:S(2)}) copy-start(f32[64,32,64]{2,1,0:T(8,128)} %copy-done.1) | copy-start | bytes 1572868
  642.6 2.8 copy-start.38
  642.6 2.9 copy-start.32
  645.4 6.6 copy-start.14
  645.4 6.6 copy-start.16
  645.4 8.5 copy-start.8
  645.4 8.5 copy-start.10
  650.1 8.6 copy-start.21
  653.9 7.9 copy-start.19
  656.0 17.6 %copy-start.11 = (f32[8,64,128]{2,1,0:T(8,128)}, f32[8,64,128]{2,1,0:T(8,128)S(1)}, u32[]{:S(2)}) copy-start(f32[8,64,128]{2,1,0:T(8,128)S(1)} %get-tuple-element.63) | copy-start | bytes 786436
  658.7 8.7 copy-start.3
  680.6 223.5 %all-to-all-start.1 = ((f32[16,16,1024]{2,1,0:T(8,128)}), f32[16,16,1024]{2,1,0:T(8,128)S(1)}, u32[]{:S(2)}, u32[]{:S(2)}) async-start(f32[16,16,1024]{2,1,0:T(8,128)} %broadcast_select_fusion), calls=%async_computation.1 | async-start | bytes 2097152 | tf_op jit(solution)/shard_map/all_to_all | solution.py:177
  690.6 2.6 copy-start.34
  690.6 2.6 copy-start.35
  693.0 1.9 copy-start.6
  694.9 15.4 %copy-start.29 = (f32[1,64,128]{2,1,0:T(8,128)S(1)}, f32[1,64,128]{2,1,0:T(8,128)}, u32[]{:S(2)}) copy-start(f32[1,64,128]{2,1,0:T(8,128)} %get-tuple-element.28) | copy-start | bytes 98308
  694.9 32.9 %copy-start.33 = (f32[16,64]{1,0:T(8,128)S(1)}, f32[16,64]{1,0:T(8,128)}, u32[]{:S(2)}) copy-start(f32[16,64]{1,0:T(8,128)} %fusion.243) | copy-start | bytes 12292
  694.9 34.9 %copy-start.28 = (f32[1,64,128]{2,1,0:T(8,128)S(1)}, f32[1,64,128]{2,1,0:T(8,128)}, u32[]{:S(2)}) copy-start(f32[1,64,128]{2,1,0:T(8,128)} %get-tuple-element.27) | copy-start | bytes 98308
  694.9 53.0 %copy-start.27 = (f32[1,64,128]{2,1,0:T(8,128)S(1)}, f32[1,64,128]{2,1,0:T(8,128)}, u32[]{:S(2)}) copy-start(f32[1,64,128]{2,1,0:T(8,128)} %get-tuple-element.26) | copy-start | bytes 98308
  694.9 75.0 %copy-start.26 = (f32[1,64,128]{2,1,0:T(8,128)S(1)}, f32[1,64,128]{2,1,0:T(8,128)}, u32[]{:S(2)}) copy-start(f32[1,64,128]{2,1,0:T(8,128)} %get-tuple-element.25) | copy-start | bytes 98308
  710.3 126.4 %copy-start.31 = (f32[128,64]{1,0:T(8,128)S(1)}, f32[128,64]{1,0:T(8,128)}, u32[]{:S(2)}) copy-start(f32[128,64]{1,0:T(8,128)} %copy.291) | copy-start | bytes 98308
  710.3 126.7 %copy-start.20 = (f32[2,64,128]{2,1,0:T(8,128)S(1)}, f32[2,64,128]{2,1,0:T(8,128)}, u32[]{:S(2)}) copy-start(f32[2,64,128]{2,1,0:T(8,128)} %get-tuple-element.59) | copy-start | bytes 196612
  710.3 127.0 %copy-start.17 = (f32[4,64,128]{2,1,0:T(8,128)S(1)}, f32[4,64,128]{2,1,0:T(8,128)}, u32[]{:S(2)}) copy-start(f32[4,64,128]{2,1,0:T(8,128)} %get-tuple-element.61) | copy-start | bytes 393220
  710.3 127.3 %copy-start.12 = (f32[8,64,128]{2,1,0:T(8,128)S(1)}, f32[8,64,128]{2,1,0:T(8,128)}, u32[]{:S(2)}) copy-start(f32[8,64,128]{2,1,0:T(8,128)} %copy-done.11) | copy-start | bytes 786436
  710.3 127.8 %copy-start.4 = (f32[16,64,128]{2,1,0:T(8,128)S(1)}, f32[16,64,128]{2,1,0:T(8,128)}, u32[]{:S(2)}) copy-start(f32[16,64,128]{2,1,0:T(8,128)} %copy-done.3) | copy-start | bytes 1572868
  725.9 3.9 collective-permute-start.1
  737.2 105.6 %copy-start.25 = (f32[1,64,128]{2,1,0:T(8,128)S(1)}, f32[1,64,128]{2,1,0:T(8,128)}, u32[]{:S(2)}) copy-start(f32[1,64,128]{2,1,0:T(8,128)} %get-tuple-element.24) | copy-start | bytes 98308
  743.0 4.9 collective-permute-start.2
  748.7 109.3 %copy-start.24 = (f32[1,64,128]{2,1,0:T(8,128)S(1)}, f32[1,64,128]{2,1,0:T(8,128)}, u32[]{:S(2)}) copy-start(f32[1,64,128]{2,1,0:T(8,128)} %get-tuple-element.23) | copy-start | bytes 98308
  761.1 8.9 collective-permute-start.3
  770.7 102.4 %copy-start.23 = (f32[1,64,128]{2,1,0:T(8,128)S(1)}, f32[1,64,128]{2,1,0:T(8,128)}, u32[]{:S(2)}) copy-start(f32[1,64,128]{2,1,0:T(8,128)} %get-tuple-element.29) | copy-start | bytes 98308
  836.1 54.0 %copy-start.22 = (f32[1,64,128]{2,1,0:T(8,128)S(1)}, f32[1,64,128]{2,1,0:T(8,128)}, u32[]{:S(2)}) copy-start(f32[1,64,128]{2,1,0:T(8,128)} %get-tuple-element.22) | copy-start | bytes 98308
  838.7 4.0 collective-permute-start.4
  850.7 7.3 collective-permute-start.5
  865.9 7.2 collective-permute-start.6
  881.1 9.0 collective-permute-start.7
  905.0 3.6 copy-start.30
where the time goes:
time: 916 us; the launch traced here: 911 us
  other arithmetic  706 us (77%)
  matrix products  73.5 us (8%)
  blocking collectives  49.2 us (5%)
  local copies, waits for them, and re-layouts  40.9 us (4%)
  starting transfers between devices  34.2 us (4%)
    another operation x43, other arithmetic, factor(): lowers = jnp.linalg.cholesky(gram_matrix)  427 us
    another operation x21, other arithmetic, factor(): inverse = jax.scipy.linalg.solve_triangular(lowers, identity, lower=True)  264 us
    all_gather x1, blocking collectives, per_device(): all_groups = lax.all_gather(group_total[None], 'group', axis=0, tiled=True)  25.1 us
    psum x1, blocking collectives, per_device(): group_total = lax.psum(moving, 'dev')  24.1 us
  transfers between devices with their start and end apart: 10, of which 3 were waited for; matrix products, arithmetic and copies ran while one was open for 45% of the time, Pallas kernels for 0%

commit v1 on v0

v1 whole, which is shorter than its diff:
```python
import functools

import jax
import jax.numpy as jnp
from jax import lax
from jax.experimental import pallas as pl
from jax.experimental.pallas import tpu as pltpu
from jax.sharding import PartitionSpec as P

f32 = jnp.float32
bf16 = jnp.bfloat16
VMEM = pl.BlockSpec(memory_space=pltpu.VMEM)
SMEM = pl.BlockSpec(memory_space=pltpu.SMEM)
soft_square = 0.01
K = 64
LEAVES = 32
NV = 16


def split(x):
    hi = x.astype(bf16)
    return hi, (x - hi.astype(f32)).astype(bf16)


def contract(a, b, rhs_lanes):
    dims = (((1,), (1 if rhs_lanes else 0,)), ((), ()))
    return lax.dot_general(a, b, dims, preferred_element_type=f32)


def mm(a, b, rhs_lanes=False):
    ah, al = split(a)
    bh, bl = split(b)
    return contract(ah, bh, rhs_lanes) + (contract(ah, bl, rhs_lanes) + contract(al, bh, rhs_lanes))


def mm6(a, b, rhs_lanes=False):
    dims = (((1,), (1 if rhs_lanes else 0,)), ((), ()))
    return lax.dot_general(
        a, b, dims, preferred_element_type=f32, precision=lax.Precision.HIGHEST
    )


def left_lanes(shape):
    return lax.broadcasted_iota(jnp.int32, shape, 1) < K


def two_blocks(slab):
    left = left_lanes(slab.shape)
    return jnp.concatenate([jnp.where(left, slab, 0.0), jnp.where(left, 0.0, slab)], axis=0)


def pack(rows):
    half = rows.shape[0] // 2
    return jnp.concatenate([rows[:half], rows[half:]], axis=1)


def call(body, outs, *args, specs=None, scratch=(), vmem=48 << 20, flops=0, aliases=None):
    return pl.pallas_call(
        body,
        out_shape=[jax.ShapeDtypeStruct(s, d) for s, d in outs],
        in_specs=specs or [VMEM] * len(args),
        out_specs=[VMEM] * len(outs),
        scratch_shapes=list(scratch),
        compiler_params=pltpu.CompilerParams(vmem_limit_bytes=vmem),
        cost_estimate=pl.CostEstimate(flops=flops, bytes_accessed=1 << 20, transcendentals=0),
        name=body.func.__name__ if isinstance(body, functools.partial) else body.__name__,
    )(*args)


def upward(counts, basis, values, pair, gram_out, joined_out, masked_out, payload_out):
    lane = lax.broadcasted_iota(jnp.int32, (NV, 2 * K), 1)
    blocks, moments = {}, {}

    def keep(parent, block, moment):
        blocks[parent] = block
        moments[parent] = moment
        gram_out[parent * K : (parent + 1) * K, :] = block[:K] + block[K:]

    for p in range(LEAVES // 2):
        cols = slice(p * 2 * K, (p + 1) * 2 * K)
        live = (lane & K - 1) < jnp.where(lane < K, counts[2 * p], counts[2 * p + 1])
        masked = jnp.where(live, values[:, cols], 0.0)
        masked_out[:, cols] = masked
        stacked = two_blocks(basis[:, cols])
        both = mm6(jnp.concatenate([stacked, masked], axis=0), stacked, True)
        keep(LEAVES // 2 + p, both[: 2 * K], both[2 * K :])
    first = LEAVES // 2
    while first > 1:
        for a in range(first, 2 * first, 2):
            weights = pair[(a - 1) * K : (a + 1) * K, :]
            left = mm6(weights[:K], blocks[a])
            right = mm6(weights[K:], blocks[a + 1])
            joined_out[(a - 1) * K : a * K, :] = left
            joined_out[a * K : (a + 1) * K, :] = right
            both = mm6(
                jnp.concatenate([left, right, moments[a], moments[a + 1]], axis=0), weights, True
            )
            off = (lax.broadcasted_iota(jnp.int32, (2 * K, 2 * K), 1) // K) == (
                lax.broadcasted_iota(jnp.int32, (2 * K, 2 * K), 0) // K
            )
            keep(
                a // 2,
                jnp.where(off, both[: 2 * K], 0.0),
                jnp.where(lane < K, both[2 * K : 2 * K + NV], both[2 * K + NV :]),
            )
        first //= 2
    weights = pair[:K, :]
    left = mm6(weights, blocks[1])
    joined_out[:K, :] = left
    both = mm6(jnp.concatenate([left, moments[1]], axis=0), weights, True)
    root = both[:K]
    gram_out[:K, :] = jnp.concatenate([root, root], axis=1)
    payload_out[: K // 2, :] = pack(root)
    payload_out[K // 2 :, :] = pack(both[K:])


def chain_level(side, own, other, pair, gram_out, joined_out, payload_out):
    flip = jnp.full(own.shape, side[0], jnp.int32) == 1
    mine, theirs = own[...], other[...]
    low = jnp.where(flip, theirs, mine)
    high = jnp.where(flip, mine, theirs)
    low_turned = pltpu.roll(low, K, 1)
    high_turned = pltpu.roll(high, K, 1)
    half = K // 2
    left = left_lanes((half, 2 * K))
    slab = jnp.concatenate(
        [
            jnp.where(left, low[:half], high_turned[:half]),
            jnp.where(left, low_turned[:half], high[:half]),
        ],
        axis=0,
    )
    gram_out[...] = slab
    small = left_lanes((NV // 2, 2 * K))
    moment = jnp.concatenate(
        [
            jnp.where(small, low[half:], high_turned[half:]),
            jnp.where(small, low_turned[half:], high[half:]),
        ],
        axis=0,
    )
    weights = pair[...]
    joined = mm6(weights, two_blocks(slab))
    joined_out[...] = joined
    both = mm6(jnp.concatenate([joined, moment], axis=0), weights, True)
    payload_out[:half, :] = pack(both[:K])
    payload_out[half:, :] = pack(both[K:])


def inverse_factors(gram, out, rows, ratios):
    pairs = gram.shape[0] // K
    width = rows.shape[2]
    step = 4
    for i in range(K):
        turned = gram[pl.ds(i, pairs, stride=K), :].T
        rows[i, :, 0:pairs] = turned[:K]
        rows[i, :, pairs : 2 * pairs] = turned[K:]
    index = lax.broadcasted_iota(jnp.int32, (K, width), 0)
    for first in range(0, K, step):
        pivots, partial = [], []
        inside = (index >= first) & (index < first + step)
        for m in range(step):
            k = first + m
            row = rows[k]
            for n in range(m):
                scale = ratios[n, k : k + 1, :]
                row = jnp.where(index == first + n, 0.0, row) - scale * partial[n]
            diagonal = row[k : k + 1, :]
            ratio = row * (1.0 / diagonal)
            ratios[m] = ratio
            row = jnp.where(index == k, 1.0, row)
            partial.append(row)
            cleared = jnp.where(inside & (index > k), 0.0, row)
            pivots.append(cleared)
            done = jnp.where(index <= k, cleared * lax.rsqrt(diagonal), 0.0)
            turned = done.T
            out[pl.ds(k, pairs, stride=K), :] = jnp.concatenate(
                [turned[:pairs, :], turned[pairs : 2 * pairs, :]], axis=1
            )

        def trailing(i, carry):
            row = jnp.where(inside, 0.0, rows[i])
            for m in range(step):
                row = row - ratios[m, pl.ds(i, 1), :] * pivots[m]
            rows[i] = row
            return carry

        if first + step < K:
            lax.fori_loop(first + step, K, trailing, 0)


def factor_batch(gram):
    (out,) = call(
        inverse_factors,
        [(gram.shape, f32)],
        gram,
        scratch=[pltpu.VMEM((K, K, 2 * K), f32), pltpu.VMEM((4, K, 2 * K), f32)],
        flops=40_000_000,
    )
    return out


def bases(basis, masked, inverse, joined, q_out, new_out, coeff_out):
    for p in range(LEAVES // 2):
        cols = slice(p * 2 * K, (p + 1) * 2 * K)
        parent = LEAVES // 2 + p
        slab = mm(inverse[parent * K : (parent + 1) * K, :], two_blocks(basis[:, cols]))
        q_out[:, cols] = slab
        coeff_out[p * NV : (p + 1) * NV, :] = mm(masked[:, cols], two_blocks(slab), True)
    for h in range(LEAVES // 2):
        inner = []
        for n in (2 * h, 2 * h + 1):
            if n > 0:
                inner.append(
                    mm(
                        joined[(n - 1) * K : n * K, :],
                        two_blocks(inverse[n * K : (n + 1) * K, :]),
                        True,
                    )
                )
        if h == 0:
            new_out[:K, :] = mm(inverse[:K, :K], inner[0])
        else:
            new_out[(2 * h - 1) * K : (2 * h + 1) * K, :] = mm(
                two_blocks(inverse[h * K : (h + 1) * K, :]), jnp.concatenate(inner, axis=0)
            )


def near_fields(near, points, masked, out, places, columns, sources):
    left = left_lanes((8, 2 * K))
    wide = left_lanes((2 * NV, 2 * K))
    count = near.shape[0] // LEAVES
    scale = float(K * count) ** (-0.5)
    for p in range(LEAVES // 2):
        cols = slice(p * 2 * K, (p + 1) * 2 * K)
        place = jnp.concatenate([points[:, cols], jnp.zeros((5, 2 * K), f32)], axis=0)
        columns[p * 2 * K : (p + 1) * 2 * K, :] = place.T
        turned = pltpu.roll(place, K, 1)
        places[2 * p] = jnp.where(left, place, turned)
        places[2 * p + 1] = jnp.where(left, turned, place)
        high, low = split(masked[:, cols])
        both = jnp.concatenate([high.astype(f32), low.astype(f32)], axis=0)
        turned = pltpu.roll(both, K, 1)
        sources[2 * p] = jnp.where(wide, both, turned).astype(bf16)
        sources[2 * p + 1] = jnp.where(wide, turned, both).astype(bf16)

    def one(leaf):
        mine = columns[pl.ds(pl.multiple_of(leaf * K, K), K), :]
        own = [jnp.broadcast_to(mine[:, c : c + 1], (K, 2 * K)) for c in range(3)]
        total = jnp.zeros((NV, K), f32)
        for n in range(0, count, 2):
            first = near[leaf * count + n]
            second = near[leaf * count + n + 1]
            place = jnp.where(left, places[first], places[second])
            square = jnp.zeros((K, 2 * K), f32)
            for c in range(3):
                gap = own[c] - place[c : c + 1, :]
                square = square + gap * gap
            high, low = split(lax.rsqrt(square + soft_square))
            source = jnp.where(wide, sources[first].astype(f32), sources[second].astype(f32)).astype(bf16)
            part = contract(source, high, True)
            total = total + (part[:NV] + part[NV:] + contract(source[:NV], low, True))
        return total * scale

    def pair(p, carry):
        out[pl.ds(pl.multiple_of(p * NV, NV), NV), :] = jnp.concatenate(
            [one(2 * p), one(2 * p + 1)], axis=1
        )
        return carry

    lax.fori_loop(0, LEAVES // 2, pair, 0)


def root_coeffs(payload, inverse, out):
    half = K // 2
    small = payload[half:, :]
    moment = jnp.concatenate([small[:, :K], small[:, K:]], axis=0)
    out[...] = pack(mm(moment, inverse[:, :K], True))


def products(
    far_row, far_side, groups, sides, counts, spread, coupling, inverse_top, chain, pair, couplings, coeffs, basis, leaf_q, near, out
):
    field = jnp.zeros((NV, K), f32)
    for f in range(2):
        row = spread[pl.ds(pl.multiple_of(groups[f] * 8, 8), 8), :]
        source = jnp.concatenate([row[:, :K], row[:, K:]], axis=0)
        high, low = split(source)
        field = field + (contract(high, coupling[f], False) + contract(low, coupling[f], False))
    value = mm(field, inverse_top[:, :K])
    for j in range(3, -1, -1):
        both = mm(value, chain[j])
        flip = jnp.full((NV, K), sides[j], jnp.int32) == 1
        value = jnp.where(flip, both[:, K:], both[:, :K])
    slabs = {1: mm(value, pair[:K, :])}
    for a in range(2, LEAVES, 2):
        both = mm(two_blocks(slabs[a // 2]), pair[(a - 1) * K : (a + 1) * K, :])
        slabs[a] = both[:NV]
        slabs[a + 1] = both[NV:]
    lane = lax.broadcasted_iota(jnp.int32, (NV, 2 * K), 1)
    left = lane < K
    for p in range(LEAVES // 2):
        cols = slice(p * 2 * K, (p + 1) * 2 * K)
        lines = []
        for leaf in (2 * p, 2 * p + 1):
            halves = []
            for f in range(4):
                s = leaf * 4 + f
                row = coeffs[pl.ds(pl.multiple_of(far_row[s], NV), NV), :]
                turn = jnp.full((NV, 2 * K), far_side[s], jnp.int32) != (f & 1)
                halves.append(jnp.where(turn, pltpu.roll(row, K, 1), row))
            lines.append(
                jnp.concatenate(
                    [jnp.where(left, halves[0], halves[1]), jnp.where(left, halves[2], halves[3])],
                    axis=1,
                )
            )
        high, low = split(jnp.concatenate(lines, axis=0))
        weights = couplings[:, :, cols].reshape(4 * K, 2 * K)
        part = contract(high, weights, False) + contract(low, weights, False)
        leaf_field = jnp.where(left, part[:NV], part[NV:])
        total = mm(
            jnp.concatenate([slabs[LEAVES // 2 + p], leaf_field], axis=1),
            jnp.concatenate([two_blocks(basis[:, cols]), two_blocks(leaf_q[:, cols])], axis=0),
        )
        live = (lane & K - 1) < jnp.where(left, counts[2 * p], counts[2 * p + 1])
        out[:, cols] = jnp.where(live, total + near[p * NV : (p + 1) * NV, :], 0.0)


def chain_bases(inverse, joined, out):
    for j in range(8):
        inner = mm(joined[j * K : (j + 1) * K, :], two_blocks(inverse[j * K : (j + 1) * K, :]), True)
        out[j] = mm(inverse[(8 + j) * K : (9 + j) * K, :K], inner)


def swapped(x, axis, distance):
    return lax.ppermute(x, axis, [(i, i ^ 1 << distance) for i in range(lax.axis_size(axis))])


def unpacked(payload):
    half = K // 2
    return jnp.concatenate([payload[:half, :K], payload[:half, K:]], axis=0)


def per_device(
    points,
    values,
    counts,
    leaf_basis,
    local_pair,
    chain_pair,
    near_leaf,
    far_peer,
    far_leaf,
    leaf_coupling,
    group_far,
    group_coupling,
):
    dev_index = lax.axis_index("dev")
    group_index = lax.axis_index("group")
    pair = local_pair.reshape(31 * K, 2 * K)
    chain = chain_pair[0]
    gram, joined, masked, payload = call(
        upward,
        [((32 * K, 2 * K), f32), ((31 * K, 2 * K), f32), (values.shape, f32), ((40, 2 * K), f32)],
        counts,
        leaf_basis,
        values,
        pair,
        specs=[SMEM, VMEM, VMEM, VMEM],
        flops=1_000_000,
    )
    sides = [
        (dev_index >> j & 1) if j < 4 else (group_index >> (j - 4) & 1) for j in range(8)
    ]
    grams, joins, payloads = [], [], [payload]
    for j in range(8):
        other = swapped(payload, "dev", j) if j < 4 else swapped(payload, "group", j - 4)
        slab, join, payload = call(
            chain_level,
            [((K, 2 * K), f32), ((K, 2 * K), f32), ((40, 2 * K), f32)],
            sides[j].reshape(1),
            payload,
            other,
            chain[j],
            specs=[SMEM, VMEM, VMEM, VMEM],
            flops=1_000_000,
        )
        grams.append(slab)
        joins.append(join)
        payloads.append(payload)
    (near,) = call(
        near_fields,
        [((LEAVES // 2 * NV, 2 * K), f32)],
        near_leaf.reshape(-1),
        points,
        masked,
        specs=[SMEM, VMEM, VMEM],
        scratch=[
            pltpu.VMEM((LEAVES, 8, 2 * K), f32),
            pltpu.VMEM((LEAVES * K, 8), f32),
            pltpu.VMEM((LEAVES, 2 * NV, 2 * K), bf16),
        ],
        flops=40_000_000,
    )
    inverse = factor_batch(gram)
    leaf_q, new_pairs, coeffs = call(
        bases,
        [(leaf_basis.shape, f32), ((31 * K, 2 * K), f32), ((LEAVES // 2 * NV, 2 * K), f32)],
        leaf_basis,
        masked,
        inverse,
        joined,
        flops=40_000_000,
    )
    all_coeffs = lax.all_gather(coeffs, "dev", axis=0, tiled=True)
    top = unpacked(payloads[4])
    top_inverse = factor_batch(jnp.tile(top, (8, 2)))[:K]
    (root,) = call(root_coeffs, [((8, 2 * K), f32)], payloads[4], top_inverse)
    spread = lax.all_to_all(
        jnp.broadcast_to(root[None], (16, 8, 2 * K)), "group", 0, 0, tiled=True
    ).reshape(128, 2 * K)
    owners = [unpacked(payloads[j + 1]) for j in range(8)]
    chain_gram = jnp.concatenate(
        grams + [jnp.concatenate([o, o], axis=1) for o in owners], axis=0
    )
    chain_inverse = factor_batch(chain_gram)
    (chain_out,) = call(
        chain_bases, [((8, K, 2 * K), f32)], chain_inverse, jnp.concatenate(joins, axis=0)
    )
    source = (dev_index + far_peer) % 16 * (LEAVES // 2 * NV) + (far_leaf >> 1) * NV
    groups = ((group_index + 1 + group_far[0]) % 16).astype(jnp.int32)
    (product,) = call(
        products,
        [(values.shape, f32)],
        source.reshape(-1),
        (far_leaf & 1).reshape(-1),
        groups,
        jnp.stack(sides[:4]),
        counts,
        spread,
        group_coupling,
        top_inverse,
        chain[:4],
        pair,
        leaf_coupling,
        all_coeffs,
        leaf_basis,
        leaf_q,
        near,
        specs=[SMEM] * 5 + [VMEM] * 10,
        flops=40_000_000,
    )
    return (leaf_q, new_pairs.reshape(31, K, 2 * K), chain_out[None], product)


def solution(mesh):
    both = ("group", "dev")
    in_specs = (
        P(None, both),
        P(None, both),
        P(both),
        P(None, both),
        P(both, None, None),
        P(both, None, None, None),
        P(both, None),
        P(both, None),
        P(both, None),
        P(None, None, both),
        P("group", None),
        P(None, None, "group"),
    )
    out_specs = (
        P(None, both),
        P(both, None, None),
        P(both, None, None, None),
        P(None, both),
    )
    return jax.shard_map(
        per_device, mesh=mesh, in_specs=in_specs, out_specs=out_specs, check_vma=False
    )
```

time: 916 us -> 156 us (0.17)
  other arithmetic: 706 us -> 6.44 us
  Pallas kernels: 0 us -> 73.8 us
  matrix products: 73.5 us -> 0 us
  blocking collectives: 49.2 us -> 0 us
  local copies, waits for them, and re-layouts: 40.9 us -> 21.6 us
  between operations: 2.28 us -> 14.4 us
    another operation x68 -> x1, other arithmetic: 691 us -> 0.08 us  [per_device(): jnp.stack(sides[:4])]
    pallas_call x0 -> x17, Pallas kernels: none -> 73.8 us  [call(): pl.pallas_call(body, out_shape=[jax.ShapeDtypeStruct(s, d) for s, d in ou...]
    dot_general x77 -> x0, matrix products: 65.1 us -> none  [the longest x14 18 us: factor(): jnp.einsum('nab,nbm->nam', inverse, stacked, precision=highest)]
    all_gather x1 -> x0, blocking collectives: 25.1 us -> none  [per_device(): all_groups = lax.all_gather(group_total[None], 'group', axis=0, tiled=True)]
    psum x1 -> x0, blocking collectives: 24.1 us -> none  [per_device(): group_total = lax.psum(moving, 'dev')]
    unnamed x79 -> x71, local copies, waits for them, and re-layouts: 3.74 us -> 16.9 us
    reshape x14 -> x3, local copies, waits for them, and re-layouts: 11.4 us -> 1.49 us  [the longest x1 0.7 us: per_device(): source.reshape(-1)]
  transfers between devices with their start and end apart: 10 -> 10, of which waited for: 3 -> 6; matrix products, arithmetic and copies ran while one was open for 45% -> 10% of each run, Pallas kernels for 0% -> 39%
where the time goes in v1:
time: 156 us; the launch traced here: 155 us
  Pallas kernels  73.8 us (47%)
  starting transfers between devices  26.3 us (17%)
  local copies, waits for them, and re-layouts  21.6 us (14%)
  between operations  14.4 us (9%)
  waiting for transfers between devices  12.1 us (8%)
  other arithmetic  6.44 us (4%)
    pallas_call x17, Pallas kernels, call(): pl.pallas_call(body, out_shape=[jax.ShapeDtypeStruct(s, d) for s, d in ou...  73.8 us
    ppermute x8, starting transfers between devices, swapped(): lax.ppermute(x, axis, [(i, i ^ 1 << distance) for i in range(lax.axis_siz...  18.9 us
    unnamed x71, local copies, waits for them, and re-layouts  16.9 us
    ppermute x8, waiting for transfers between devices, swapped(): lax.ppermute(x, axis, [(i, i ^ 1 << distance) for i in range(lax.axis_siz...  12 us
    all_to_all x1, starting transfers between devices, per_device(): lax.all_to_all(jnp.broadcast_to(root[None], (16, 8, 2 * K)), 'group', 0,...  7.33 us
    unnamed x7, other arithmetic  3.89 us
  transfers between devices with their start and end apart: 10, of which 6 were waited for; matrix products, arithmetic and copies ran while one was open for 10% of the time, Pallas kernels for 39%

profile of v1, /device:TPU:4, one launch (start us, length us, event | category | flops | bytes accessed | tf_op | source)
XLA Modules:
  0.0 154.5 jit_solution(188444369172921148)
XLA Ops:
  7.2 1.0 copy-done
  8.3 1.2 copy-done.2
  9.5 0.9 copy-done.9
  10.4 0.7 copy-done.17
  11.0 7.2 %upward.1 = (f32[2048,128]{1,0:T(8,128)S(1)}, f32[1984,128]{1,0:T(8,128)S(1)}, f32[16,2048]{1,0:T(8,128)S(1)}, f32[40,128]{1,0:T(8,128)S(1)}) custom-call(s32[32]{0:T(128)S(1)} %copy-done.17, f32[64,2048]{1,0:T(8,128)S(1)} %copy-done, f32[16,2048]{1,0:T(8,128)S(1)} %copy-done.9, f32[1984,128]{1,0:T(8,128)S(1)} %bitcast.32), custom_call_target="tpu_custom_call" | custom-call | flops 1000000 | bytes 1048576 | tf_op jit(solution)/shard_map/upward/pallas_call | solution.py:58
  18.3 0.3 collective-permute-start
  18.6 12.6 %inverse_factors.3.inverse = f32[2048,128]{1,0:T(8,128)S(1)} custom-call(f32[2048,128]{1,0:T(8,128)S(1)} %get-tuple-element.36.gram), custom_call_target="tpu_custom_call" | custom-call | flops 40000000 | bytes 1048576 | tf_op jit(solution)/shard_map/inverse_factors/pallas_call | solution.py:58
  31.2 7.5 %bases.1 = (f32[64,2048]{1,0:T(8,128)}, f32[1984,128]{1,0:T(8,128)}, f32[256,128]{1,0:T(8,128)}) custom-call(f32[64,2048]{1,0:T(8,128)S(1)} %copy-done.1, f32[16,2048]{1,0:T(8,128)S(1)} %get-tuple-element.35.masked, f32[2048,128]{1,0:T(8,128)S(1)} %inverse_factors.3.inverse, f32[1984,128]{1,0:T(8,128)S(1)} %get-tuple-element.37.joined), custom_call_target="tpu_custom_call" | custom-call | flops 40000000 | bytes 1048576 | tf_op jit(solution)/shard_map/bases/pallas_call | solution.py:58
  38.7 0.6 slice_bitcast_fusion.1
  39.4 0.5 and_select_fusion.groups
  40.1 0.7 reshape.81.far_row
  40.9 0.7 reshape.82.far_side
  41.8 9.2 %near_fields.1.near = f32[256,128]{1,0:T(8,128)S(1)} custom-call(s32[384]{0:T(512)S(1)} %reshape.84.near, f32[3,2048]{1,0:T(4,128)S(1)} %copy-done.14, f32[16,2048]{1,0:T(8,128)S(1)} %get-tuple-element.35.masked), custom_call_target="tpu_custom_call" | custom-call | flops 40000000 | bytes 1048576 | tf_op jit(solution)/shard_map/near_fields/pallas_call | solution.py:58
  51.0 0.5 chain_level.8
  51.5 2.0 %collective-permute-start.1 = (f32[40,128]{1,0:T(8,128)S(1)}, f32[40,128]{1,0:T(8,128)S(1)}, u32[]{:S(2)}, u32[]{:S(2)}) collective-permute-start(f32[40,128]{1,0:T(8,128)S(1)} %get-tuple-element.42.own), channel_id=1, source_target_pairs={{0,2},{1,3},{2,0},{3,1},{4,6},{5,7},{6,4},{7,5},{8,10},{9,11},{10,... | collective-permute-start | bytes 61448 | tf_op jit(solution)/shard_map/ppermute | solution.py:337
  53.6 0.6 pad_maximum_fusion
  54.2 1.5 collective-permute-done.1.other
  55.7 0.5 chain_level.9
  56.2 3.1 %collective-permute-start.2 = (f32[40,128]{1,0:T(8,128)S(1)}, f32[40,128]{1,0:T(8,128)S(1)}, u32[]{:S(2)}, u32[]{:S(2)}) collective-permute-start(f32[40,128]{1,0:T(8,128)S(1)} %get-tuple-element.44.own), channel_id=1, source_target_pairs={{0,4},{1,5},{2,6},{3,7},{4,0},{5,1},{6,2},{7,3},{8,12},{9,13},{10,... | collective-permute-start | bytes 61448 | tf_op jit(solution)/shard_map/ppermute | solution.py:337
  59.4 0.6 pad_maximum_fusion.1
  60.0 1.6 %collective-permute-done.2.other = f32[40,128]{1,0:T(8,128)S(1)} collective-permute-done((f32[40,128]{1,0:T(8,128)S(1)}, f32[40,128]{1,0:T(8,128)S(1)}, u32[]{:S(2)}, u32[]{:S(2)}) %collective-permute-start.2) | collective-permute-done | bytes 20512 | tf_op jit(solution)/shard_map/ppermute | solution.py:337
  61.6 0.5 chain_level.10
  62.1 6.8 %collective-permute-start.3 = (f32[40,128]{1,0:T(8,128)S(1)}, f32[40,128]{1,0:T(8,128)S(1)}, u32[]{:S(2)}, u32[]{:S(2)}) collective-permute-start(f32[40,128]{1,0:T(8,128)S(1)} %get-tuple-element.46.own), channel_id=1, source_target_pairs={{0,8},{1,9},{2,10},{3,11},{4,12},{5,13},{6,14},{7,15},{8,0},{9,1},... | collective-permute-start | bytes 61448 | tf_op jit(solution)/shard_map/ppermute | solution.py:337
  68.9 0.6 pad_maximum_fusion.2
  69.5 1.5 collective-permute-done.3.other
  71.0 0.5 chain_level.11
  71.6 1.5 collective-permute-start.4
  73.3 0.3 tile.10.gram
  73.8 11.7 %inverse_factors.5 = f32[512,128]{1,0:T(8,128)S(1)} custom-call(f32[512,128]{1,0:T(8,128)S(1)} %tile.10.gram), custom_call_target="tpu_custom_call" | custom-call | flops 40000000 | bytes 1048576 | tf_op jit(solution)/shard_map/inverse_factors/pallas_call | solution.py:58
  85.5 0.2 root_coeffs.1
  85.7 0.7 broadcast_in_dim.10
  86.4 7.3 %all-to-all-start = ((f32[16,8,128]{2,1,0:T(8,128)}), f32[16,8,128]{2,1,0:T(8,128)S(1)}, u32[]{:S(2)}, u32[]{:S(2)}) async-start(f32[16,8,128]{2,1,0:T(8,128)} %broadcast_in_dim.10), calls=%async_computation | async-start | bytes 131072 | tf_op jit(solution)/shard_map/all_to_all | solution.py:420
  93.7 0.9 constant_dynamic-update-slice_fusion.12
  94.7 1.4 constant_dynamic-update-slice_fusion.20
  96.0 0.8 copy-done.12
  96.8 0.5 chain_level.12
  97.6 0.6 constant_dynamic-update-slice_fusion.19
  98.2 4.5 %collective-permute-done.5.other = f32[40,128]{1,0:T(8,128)S(1)} collective-permute-done((f32[40,128]{1,0:T(8,128)S(1)}, f32[40,128]{1,0:T(8,128)S(1)}, u32[]{:S(2)}, u32[]{:S(2)}) %collective-permute-start.5) | collective-permute-done | bytes 20512 | tf_op jit(solution)/shard_map/ppermute | solution.py:337
  102.7 0.8 copy-done.11
  103.4 0.5 chain_level.13
  103.9 1.6 %collective-permute-start.6 = (f32[40,128]{1,0:T(8,128)S(1)}, f32[40,128]{1,0:T(8,128)S(1)}, u32[]{:S(2)}, u32[]{:S(2)}) collective-permute-start(f32[40,128]{1,0:T(8,128)S(1)} %get-tuple-element.52.own), channel_id=1, source_target_pairs={{0,64},{16,80},{32,96},{48,112},{64,0},{80,16},{96,32},{112,48},{1... | collective-permute-start | bytes 61448 | tf_op jit(solution)/shard_map/ppermute | solution.py:337
  105.6 0.6 constant_dynamic-update-slice_fusion.18
  106.2 1.6 %collective-permute-done.6.other = f32[40,128]{1,0:T(8,128)S(1)} collective-permute-done((f32[40,128]{1,0:T(8,128)S(1)}, f32[40,128]{1,0:T(8,128)S(1)}, u32[]{:S(2)}, u32[]{:S(2)}) %collective-permute-start.6) | collective-permute-done | bytes 20512 | tf_op jit(solution)/shard_map/ppermute | solution.py:337
  107.8 0.8 copy-done.10
  108.6 0.5 chain_level.14
  109.1 3.5 %collective-permute-start.7 = (f32[40,128]{1,0:T(8,128)S(1)}, f32[40,128]{1,0:T(8,128)S(1)}, u32[]{:S(2)}, u32[]{:S(2)}) collective-permute-start(f32[40,128]{1,0:T(8,128)S(1)} %get-tuple-element.54.own), channel_id=1, source_target_pairs={{0,128},{16,144},{32,160},{48,176},{64,192},{80,208},{96,224},{112... | collective-permute-start | bytes 61448 | tf_op jit(solution)/shard_map/ppermute | solution.py:337
  112.7 0.6 constant_dynamic-update-slice_fusion.17
  113.3 1.4 collective-permute-done.7.other
  114.7 0.5 chain_level.15
  115.3 0.9 constant_dynamic-update-slice_fusion.7
  116.2 0.9 constant_dynamic-update-slice_fusion.6
  117.1 0.9 constant_dynamic-update-slice_fusion.5
  118.0 0.9 constant_dynamic-update-slice_fusion.4
  119.3 12.4 %inverse_factors.4.inverse = f32[1024,128]{1,0:T(8,128)S(1)} custom-call(f32[1024,128]{1,0:T(8,128)S(1)} %constant_dynamic-update-slice_fusion.gram), custom_call_target="tpu_custom_call" | custom-call | flops 40000000 | bytes 1048576 | tf_op jit(solution)/shard_map/inverse_factors/pallas_call | solution.py:58
  131.7 0.6 constant_dynamic-update-slice_fusion.16.joined
  132.4 0.9 copy-done.8
  133.3 2.8 %chain_bases.1 = f32[8,64,128]{2,1,0:T(8,128)} custom-call(f32[1024,128]{1,0:T(8,128)S(1)} %inverse_factors.4.inverse, f32[512,128]{1,0:T(8,128)S(1)} %copy-done.8), custom_call_target="tpu_custom_call" | custom-call | bytes 1048576 | tf_op jit(solution)/shard_map/chain_bases/pallas_call | solution.py:58
  136.2 1.6 %copy-done.4 = f32[4096,128]{1,0:T(8,128)S(1)} copy-done((f32[4096,128]{1,0:T(8,128)S(1)}, f32[4096,128]{1,0:T(8,128)}, u32[]{:S(2)}) %copy-start.4) | copy-done | bytes 2097176
  137.8 1.0 copy-done.6
  138.8 0.8 copy-done.13
  139.6 0.7 copy-done.19
  140.2 0.7 copy-done.20
  140.9 0.6 copy-done.21
  141.5 6.2 %products.1 = f32[16,2048]{1,0:T(8,128)} custom-call(s32[128]{0:T(128)S(1)} %copy-done.19, s32[128]{0:T(128)S(1)} %copy-done.20, s32[2]{0:T(128)S(1)} %copy-done.21, s32[4]{0:T(128)S(1)} %pad_add_fusion.sides, s32[32]{0:T(128)S(1)} %copy-done.18, f32[128,128]{1,0:T(8,128)S(1)} %bitcast.34, bf16[2,64,64]{2,1,0:T(8,128)(2,1)S(1)} %copy-done.13, ...), custom_call_target="tpu_custom_call" | custom-call | flops 40000000 | bytes 1048576 | tf_op jit(solution)/shard_map/products/pallas_call | solution.py:58
  (84 shorter events, 2.2 us)
Async XLA Ops:
  7.2 129.0 %all-gather.2.cloned.1.call-start = ((), (), s32[]{:S(2)}) async-start(), calls=%async_computation.1 | async-start | bytes 2228224 | tf_op jit(solution)/shard_map/all_gather | solution.py:416
  7.2 1.0 copy-start
  8.3 1.2 copy-start.2
  9.5 0.9 copy-start.9
  10.4 0.7 copy-start.17
  11.0 20.2 %copy-start.1 = (f32[64,2048]{1,0:T(8,128)S(1)}, f32[64,2048]{1,0:T(8,128)}, u32[]{:S(2)}) copy-start(f32[64,2048]{1,0:T(8,128)} %basis.5) | copy-start | bytes 1572868
  18.3 32.7 %collective-permute-start = (f32[40,128]{1,0:T(8,128)S(1)}, f32[40,128]{1,0:T(8,128)S(1)}, u32[]{:S(2)}, u32[]{:S(2)}) collective-permute-start(f32[40,128]{1,0:T(8,128)S(1)} %get-tuple-element.40.own), channel_id=1, source_target_pairs={{0,1},{1,0},{2,3},{3,2},{4,5},{5,4},{6,7},{7,6},{8,9},{9,8},{10,11... | collective-permute-start | bytes 61448 | tf_op jit(solution)/shard_map/ppermute | solution.py:337
  18.5 20.1 %copy-start.22 = (f32[1,8,64,128]{3,2,1,0:T(8,128)S(1)}, f32[1,8,64,128]{3,2,1,0:T(8,128)}, u32[]{:S(2)}) copy-start(f32[1,8,64,128]{3,2,1,0:T(8,128)} %param.17) | copy-start | bytes 786436
  31.1 8.2 %copy-start.25 = (s32[32,4]{0,1:T(4,128)S(1)}, s32[32,4]{0,1:T(4,128)}, u32[]{:S(2)}) copy-start(s32[32,4]{0,1:T(4,128)} %param.20) | copy-start | bytes 1540
  31.1 8.2 %copy-start.26 = (s32[32,4]{0,1:T(4,128)S(1)}, s32[32,4]{0,1:T(4,128)}, u32[]{:S(2)}) copy-start(s32[32,4]{0,1:T(4,128)} %param.19) | copy-start | bytes 1540
  31.1 8.3 %copy-start.27 = (s32[1,2]{1,0:T(1,128)S(1)}, s32[1,2]{1,0:T(1,128)}, u32[]{:S(2)}) copy-start(s32[1,2]{1,0:T(1,128)} %param.22) | copy-start | bytes 28
  31.2 10.4 %copy-start.24 = (s32[32,12]{0,1:T(8,128)S(1)}, s32[32,12]{0,1:T(8,128)}, u32[]{:S(2)}) copy-start(s32[32,12]{0,1:T(8,128)} %param.18) | copy-start | bytes 4612
  31.2 10.6 %copy-start.14 = (f32[3,2048]{1,0:T(4,128)S(1)}, f32[3,2048]{1,0:T(4,128)}, u32[]{:S(2)}) copy-start(f32[3,2048]{1,0:T(4,128)} %points.1) | copy-start | bytes 73732
  51.5 4.2 %collective-permute-start.1 = (f32[40,128]{1,0:T(8,128)S(1)}, f32[40,128]{1,0:T(8,128)S(1)}, u32[]{:S(2)}, u32[]{:S(2)}) collective-permute-start(f32[40,128]{1,0:T(8,128)S(1)} %get-tuple-element.42.own), channel_id=1, source_target_pairs={{0,2},{1,3},{2,0},{3,1},{4,6},{5,7},{6,4},{7,5},{8,10},{9,11},{10,... | collective-permute-start | bytes 61448 | tf_op jit(solution)/shard_map/ppermute | solution.py:337
  56.2 5.4 %collective-permute-start.2 = (f32[40,128]{1,0:T(8,128)S(1)}, f32[40,128]{1,0:T(8,128)S(1)}, u32[]{:S(2)}, u32[]{:S(2)}) collective-permute-start(f32[40,128]{1,0:T(8,128)S(1)} %get-tuple-element.44.own), channel_id=1, source_target_pairs={{0,4},{1,5},{2,6},{3,7},{4,0},{5,1},{6,2},{7,3},{8,12},{9,13},{10,... | collective-permute-start | bytes 61448 | tf_op jit(solution)/shard_map/ppermute | solution.py:337
  62.1 8.9 %collective-permute-start.3 = (f32[40,128]{1,0:T(8,128)S(1)}, f32[40,128]{1,0:T(8,128)S(1)}, u32[]{:S(2)}, u32[]{:S(2)}) collective-permute-start(f32[40,128]{1,0:T(8,128)S(1)} %get-tuple-element.46.own), channel_id=1, source_target_pairs={{0,8},{1,9},{2,10},{3,11},{4,12},{5,13},{6,14},{7,15},{8,0},{9,1},... | collective-permute-start | bytes 61448 | tf_op jit(solution)/shard_map/ppermute | solution.py:337
  69.5 3.6 %copy-start.7 = (f32[512,128]{1,0:T(8,128)}, f32[512,128]{1,0:T(8,128)S(1)}, u32[]{:S(2)}) copy-start(f32[512,128]{1,0:T(8,128)S(1)} %constant_dynamic-update-slice_fusion.21) | copy-start | bytes 786436
  71.5 1.7 %copy-start.15 = (f32[64,128]{1,0:T(8,128)}, f32[64,128]{1,0:T(8,128)S(1)}, u32[]{:S(2)}) copy-start(f32[64,128]{1,0:T(8,128)S(1)} %get-tuple-element.60) | copy-start | bytes 98308
  71.5 1.7 %copy-start.16 = (f32[64,128]{1,0:T(8,128)}, f32[64,128]{1,0:T(8,128)S(1)}, u32[]{:S(2)}) copy-start(f32[64,128]{1,0:T(8,128)S(1)} %get-tuple-element.47) | copy-start | bytes 98308
  71.6 24.5 %collective-permute-start.4 = (f32[40,128]{1,0:T(8,128)S(1)}, f32[40,128]{1,0:T(8,128)S(1)}, u32[]{:S(2)}, u32[]{:S(2)}) collective-permute-start(f32[40,128]{1,0:T(8,128)S(1)} %get-tuple-element.48.own.payload), channel_id=1, source_target_pairs={{0,16},{16,0},{32,48},{48,32},{64,80},{80,64},{96,112},{112,96},{1... | collective-permute-start | bytes 61448 | tf_op jit(solution)/shard_map/ppermute | solution.py:337
  73.2 0.6 copy-start.23
  86.4 49.8 %copy-start.18 = (s32[32]{0:T(128)S(1)}, s32[32]{0:T(128)}, u32[]{:S(2)}) copy-start(s32[32]{0:T(128)} %counts.3) | copy-start | bytes 388
  86.4 49.8 %all-to-all-start = ((f32[16,8,128]{2,1,0:T(8,128)}), f32[16,8,128]{2,1,0:T(8,128)S(1)}, u32[]{:S(2)}, u32[]{:S(2)}) async-start(f32[16,8,128]{2,1,0:T(8,128)} %broadcast_in_dim.10), calls=%async_computation | async-start | bytes 131072 | tf_op jit(solution)/shard_map/all_to_all | solution.py:420
  93.7 42.4 %copy-start.3 = (f32[31,64,128]{2,1,0:T(8,128)S(1)}, f32[31,64,128]{2,1,0:T(8,128)}, u32[]{:S(2)}) copy-start(f32[31,64,128]{2,1,0:T(8,128)} %param.16) | copy-start | bytes 3047428
  93.7 42.4 %copy-start.5 = (bf16[4,64,2048]{2,1,0:T(8,128)(2,1)S(1)}, bf16[4,64,2048]{2,1,0:T(8,128)(2,1)}, u32[]{:S(2)}) copy-start(bf16[4,64,2048]{2,1,0:T(8,128)(2,1)} %couplings.1) | copy-start | bytes 3145732
  96.0 0.8 copy-start.12
  97.3 5.4 %collective-permute-start.5 = (f32[40,128]{1,0:T(8,128)S(1)}, f32[40,128]{1,0:T(8,128)S(1)}, u32[]{:S(2)}, u32[]{:S(2)}) collective-permute-start(f32[40,128]{1,0:T(8,128)S(1)} %get-tuple-element.50.own), channel_id=1, source_target_pairs={{0,32},{16,48},{32,0},{48,16},{64,96},{80,112},{96,64},{112,80},{1... | collective-permute-start | bytes 61448 | tf_op jit(solution)/shard_map/ppermute | solution.py:337
  102.7 0.8 copy-start.11
  103.9 3.9 %collective-permute-start.6 = (f32[40,128]{1,0:T(8,128)S(1)}, f32[40,128]{1,0:T(8,128)S(1)}, u32[]{:S(2)}, u32[]{:S(2)}) collective-permute-start(f32[40,128]{1,0:T(8,128)S(1)} %get-tuple-element.52.own), channel_id=1, source_target_pairs={{0,64},{16,80},{32,96},{48,112},{64,0},{80,16},{96,32},{112,48},{1... | collective-permute-start | bytes 61448 | tf_op jit(solution)/shard_map/ppermute | solution.py:337
  107.8 0.8 copy-start.10
  109.1 5.6 %collective-permute-start.7 = (f32[40,128]{1,0:T(8,128)S(1)}, f32[40,128]{1,0:T(8,128)S(1)}, u32[]{:S(2)}, u32[]{:S(2)}) collective-permute-start(f32[40,128]{1,0:T(8,128)S(1)} %get-tuple-element.54.own), channel_id=1, source_target_pairs={{0,128},{16,144},{32,160},{48,176},{64,192},{80,208},{96,224},{112... | collective-permute-start | bytes 61448 | tf_op jit(solution)/shard_map/ppermute | solution.py:337
  132.4 0.9 copy-start.8
  136.2 1.6 %copy-start.4 = (f32[4096,128]{1,0:T(8,128)S(1)}, f32[4096,128]{1,0:T(8,128)}, u32[]{:S(2)}) copy-start(f32[4096,128]{1,0:T(8,128)} %all-gather.2.cloned.1.call-done.coeffs) | copy-start | bytes 6291460
  137.8 1.0 copy-start.6
  138.8 0.8 copy-start.13
  139.6 0.7 copy-start.19
  140.2 0.7 copy-start.20
  140.9 0.6 copy-start.21
Sparse Core Ops, SparseCore 0:
  38.8 42.5 all-gather.1

commit v2 on v1

v2 whole, which is shorter than its diff:
```python
import functools

import jax
import jax.numpy as jnp
from jax import lax
from jax.experimental import pallas as pl
from jax.experimental.pallas import tpu as pltpu
from jax.sharding import PartitionSpec as P

f32 = jnp.float32
bf16 = jnp.bfloat16
VMEM = pl.BlockSpec(memory_space=pltpu.VMEM)
SMEM = pl.BlockSpec(memory_space=pltpu.SMEM)
soft_square = 0.01
K = 64
LEAVES = 32
NV = 16


def split(x):
    hi = x.astype(bf16)
    return hi, (x - hi.astype(f32)).astype(bf16)


def contract(a, b, rhs_lanes):
    dims = (((1,), (1 if rhs_lanes else 0,)), ((), ()))
    return lax.dot_general(a, b, dims, preferred_element_type=f32)


def mm(a, b, rhs_lanes=False):
    ah, al = split(a)
    bh, bl = split(b)
    return contract(ah, bh, rhs_lanes) + (contract(ah, bl, rhs_lanes) + contract(al, bh, rhs_lanes))


def mm6(a, b, rhs_lanes=False):
    dims = (((1,), (1 if rhs_lanes else 0,)), ((), ()))
    return lax.dot_general(
        a, b, dims, preferred_element_type=f32, precision=lax.Precision.HIGHEST
    )


gram_mm = mm


def left_lanes(shape):
    return lax.broadcasted_iota(jnp.int32, shape, 1) < K


def two_blocks(slab):
    left = left_lanes(slab.shape)
    return jnp.concatenate([jnp.where(left, slab, 0.0), jnp.where(left, 0.0, slab)], axis=0)


def pack(rows):
    half = rows.shape[0] // 2
    return jnp.concatenate([rows[:half], rows[half:]], axis=1)


def call(body, outs, *args, specs=None, scratch=(), after=(), us=0.02, vmem=16):
    given = len(args)

    def kernel(*refs):
        body(*refs[:given], *refs[given + len(after) :])

    return pl.pallas_call(
        kernel,
        out_shape=[jax.ShapeDtypeStruct(s, d) for s, d in outs],
        in_specs=(specs or [VMEM] * given) + [pl.BlockSpec(memory_space=pl.ANY)] * len(after),
        out_specs=[VMEM] * len(outs),
        scratch_shapes=list(scratch),
        compiler_params=pltpu.CompilerParams(vmem_limit_bytes=vmem << 20),
        cost_estimate=pl.CostEstimate(
            flops=int(us * 1e9), bytes_accessed=1 << 18, transcendentals=0
        ),
        name=body.func.__name__ if isinstance(body, functools.partial) else body.__name__,
    )(*args, *after)


def unpack(packed):
    return jnp.concatenate([packed[:, :K], packed[:, K:]], axis=0)


def side_by_side(low, high):
    left = left_lanes(low.shape)
    return jnp.concatenate(
        [
            jnp.where(left, low, pltpu.roll(high, K, 1)),
            jnp.where(left, pltpu.roll(low, K, 1), high),
        ],
        axis=0,
    )


def chosen(side, zero, one):
    return jnp.where(jnp.full(zero.shape, side, jnp.int32) == 1, one, zero)


def packed_level(side, own, other, weights):
    low, high = chosen(side, own, other), chosen(side, other, own)
    slab = side_by_side(low[:32], high[:32])
    joined = gram_mm(weights, two_blocks(slab))
    both = gram_mm(
        jnp.concatenate([joined, side_by_side(low[32:40], high[32:40])], axis=0), weights, True
    )
    return slab, joined, jnp.concatenate([pack(both[:K]), pack(both[K:])], axis=0)


def packed_share(side, own, weights):
    mine = chosen(side, weights[:, :K], weights[:, K:])
    inner = gram_mm(mine, unpack(own[:32]))
    both = gram_mm(jnp.concatenate([inner, unpack(own[32:40])], axis=0), mine, True)
    return jnp.concatenate([pack(both[:K]), pack(both[K:])], axis=0)


def upward(
    counts, sides, basis_in, values_in, pair_in, chain_in, gram_out, joined_out, masked_out, payload_out, share_out, basis, values, pair, chain, sems
):
    copies = [
        pltpu.make_async_copy(source, target, sems.at[n])
        for n, (source, target) in enumerate(
            ((values_in, values), (basis_in, basis), (pair_in, pair), (chain_in.at[pl.ds(0, K)], chain))
        )
    ]
    for copy in copies:
        copy.start()
    copies[0].wait()
    copies[1].wait()
    lane = lax.broadcasted_iota(jnp.int32, (NV, 2 * K), 1)
    blocks, moments = {}, {}

    def keep(parent, block, moment):
        blocks[parent] = block
        moments[parent] = moment
        gram_out[parent * K : (parent + 1) * K, :] = block[:K] + block[K:]

    for p in range(LEAVES // 2):
        cols = slice(p * 2 * K, (p + 1) * 2 * K)
        live = (lane & K - 1) < jnp.where(lane < K, counts[2 * p], counts[2 * p + 1])
        masked = jnp.where(live, values[:, cols], 0.0)
        masked_out[:, cols] = masked
        stacked = two_blocks(basis[:, cols])
        both = gram_mm(jnp.concatenate([stacked, masked], axis=0), stacked, True)
        keep(LEAVES // 2 + p, both[: 2 * K], both[2 * K :])
    copies[2].wait()
    copies[3].wait()
    first = LEAVES // 2
    while first > 1:
        for a in range(first, 2 * first, 2):
            weights = pair[(a - 1) * K : (a + 1) * K, :]
            left = gram_mm(weights[:K], blocks[a])
            right = gram_mm(weights[K:], blocks[a + 1])
            joined_out[(a - 1) * K : a * K, :] = left
            joined_out[a * K : (a + 1) * K, :] = right
            both = gram_mm(
                jnp.concatenate([left, right, moments[a], moments[a + 1]], axis=0), weights, True
            )
            off = (lax.broadcasted_iota(jnp.int32, (2 * K, 2 * K), 1) // K) == (
                lax.broadcasted_iota(jnp.int32, (2 * K, 2 * K), 0) // K
            )
            keep(
                a // 2,
                jnp.where(off, both[: 2 * K], 0.0),
                jnp.where(lane < K, both[2 * K : 2 * K + NV], both[2 * K + NV :]),
            )
        first //= 2
    weights = pair[:K, :]
    left = gram_mm(weights, blocks[1])
    joined_out[:K, :] = left
    both = gram_mm(jnp.concatenate([left, moments[1]], axis=0), weights, True)
    root = both[:K]
    gram_out[:K, :] = jnp.concatenate([root, root], axis=1)
    payload = jnp.concatenate([pack(root), pack(both[K:])], axis=0)
    payload_out[...] = payload
    share_out[...] = packed_share(sides[0], payload, chain[:K, :])


def two_levels(level, sides, own, near, far, farther, chain, slab_out, joined_out, *sends):
    start = own[:40, :]
    slab, joined, node = packed_level(sides[level], start, near[:40, :], chain[level * K : (level + 1) * K, :])
    slab_out[:K, :] = slab
    joined_out[:K, :] = joined
    rest = far[:40, :] + farther[:40, :]
    slab, joined, node = packed_level(sides[level + 1], node, rest, chain[(level + 1) * K : (level + 2) * K, :])
    slab_out[K:, :] = slab
    joined_out[K:, :] = joined
    if level < 6:
        share = packed_share(sides[level + 2], node, chain[(level + 2) * K : (level + 3) * K, :])
    if level == 0:
        sends[0][...] = node
        sends[1][...] = share
    elif level == 2:
        sends[0][...] = node
        sends[1][:32, :] = share[:32]
        sends[1][32:, :] = node
    elif level == 4:
        sends[0][:32, :] = node[:32]
        sends[1][:32, :] = share[:32]
        for send in sends:
            send[32:72, :] = start
            send[72:112, :] = near[...]
            send[112:152, :] = far[32:, :]
            send[152:, :] = farther[32:, :]
    else:
        sends[0][...] = node


def last_levels(
    sides, places, own, near, far, farther, chain, slabs0, slabs1, slabs2, joins0, joins1, joins2,
    gram_out, joined_out, moment_out, held, slabs, joins, top
):
    two_levels(6, sides, own, near, far, farther, chain, slabs, joins, top)
    for n, ref in enumerate((slabs0, slabs1, slabs2, slabs)):
        gram_out[2 * n * K : 2 * (n + 1) * K, :] = ref[...]
    for n, ref in enumerate((joins0, joins1, joins2, joins)):
        joined_out[2 * n * K : 2 * (n + 1) * K, :] = ref[...]
    for n, ref in enumerate((own, near, far, farther)):
        held[n * 160 : (n + 1) * 160, :] = ref[32:, :]
    sources = [held[pl.ds(pl.multiple_of(places[f] * 40, 8), 40), :] for f in range(2)]
    gram_out[8 * K : 9 * K, :] = side_by_side(top[:32, :], sources[0][:32])
    gram_out[9 * K : 10 * K, :] = side_by_side(sources[1][:32], sources[1][:32])
    for n in range(10, 16):
        gram_out[n * K : (n + 1) * K, :] = slabs[:K, :]
    moment_out[...] = side_by_side(sources[0][32:], sources[1][32:])


def inverse_factors(gram, out, rows, ratios):
    pairs = gram.shape[0] // K
    width = rows.shape[2]
    step, tile = 4, 8
    for i in range(K):
        turned = gram[pl.ds(i, pairs, stride=K), :].T
        rows[i, :, 0:pairs] = turned[:K]
        rows[i, :, pairs : 2 * pairs] = turned[K:]
    index = lax.broadcasted_iota(jnp.int32, (K, width), 0)
    near_index = lax.broadcasted_iota(jnp.int32, (tile, width), 0)
    for first in range(0, K, step):
        pivots, partial = [], []
        home = first // tile
        inside = (index >= first) & (index < first + step)
        for m in range(step):
            k = first + m
            row = rows[k]
            for n in range(m):
                scale = ratios[first + n, k : k + 1, :]
                row = jnp.where(index == first + n, 0.0, row) - scale * partial[n]
            diagonal = row[k : k + 1, :]
            ratios[k] = row * (1.0 / diagonal)
            row = jnp.where(index == k, 1.0, row)
            partial.append(row)
            pivots.append(jnp.where(inside & (index > k), 0.0, row))
            done = jnp.where(index <= k, row * lax.rsqrt(diagonal), 0.0)
            turned = done[:, : 2 * pairs].T
            out[pl.ds(k, pairs, stride=K), :] = jnp.concatenate(
                [turned[:pairs, :], turned[pairs:, :]], axis=1
            )
        start = first % tile
        cleared = (near_index >= start) & (near_index < start + step)
        for i in range(first + step, K):
            scales = [
                jnp.broadcast_to(ratios[first + m, i : i + 1, :], (tile, width))
                for m in range(step)
            ]
            for g in range(K // tile):
                if home < g < i // tile:
                    continue
                part = slice(g * tile, (g + 1) * tile)
                row = rows[i, part, :]
                if g == home:
                    row = jnp.where(cleared, 0.0, row)
                for m in range(step):
                    row = row - scales[m] * pivots[m][part]
                rows[i, part, :] = row


def factor_batch(gram, us=0.02):
    (out,) = call(
        inverse_factors,
        [(gram.shape, f32)],
        gram,
        scratch=[pltpu.VMEM((K, K, 2 * K), f32), pltpu.VMEM((K, K, 2 * K), f32)],
        us=us,
    )
    return out


def bases(basis, masked, inverse, q_out, coeff_out):
    for p in range(LEAVES // 2):
        cols = slice(p * 2 * K, (p + 1) * 2 * K)
        parent = LEAVES // 2 + p
        slab = mm(inverse[parent * K : (parent + 1) * K, :], two_blocks(basis[:, cols]))
        q_out[:, cols] = slab
        coeff_out[p * NV : (p + 1) * NV, :] = mm(masked[:, cols], two_blocks(slab), True)


def transfers(inverse, joined, new_out):
    for h in range(LEAVES // 2):
        inner = []
        for n in (2 * h, 2 * h + 1):
            if n > 0:
                inner.append(
                    mm(
                        joined[(n - 1) * K : n * K, :],
                        two_blocks(inverse[n * K : (n + 1) * K, :]),
                        True,
                    )
                )
        if h == 0:
            new_out[:K, :] = mm(inverse[:K, :K], inner[0])
        else:
            new_out[(2 * h - 1) * K : (2 * h + 1) * K, :] = mm(
                two_blocks(inverse[h * K : (h + 1) * K, :]), jnp.concatenate(inner, axis=0)
            )


def near_fields(start, stop, near, points, masked, out, places, columns, sources):
    left = left_lanes((8, 2 * K))
    wide = left_lanes((2 * NV, 2 * K))
    count = near.shape[0] // LEAVES
    scale = float(K * count) ** (-0.5)
    for p in range(LEAVES // 2):
        cols = slice(p * 2 * K, (p + 1) * 2 * K)
        place = jnp.concatenate([points[:, cols], jnp.zeros((5, 2 * K), f32)], axis=0)
        columns[p * 2 * K : (p + 1) * 2 * K, :] = place.T
        turned = pltpu.roll(place, K, 1)
        places[2 * p] = jnp.where(left, place, turned)
        places[2 * p + 1] = jnp.where(left, turned, place)
        high, low = split(masked[:, cols])
        both = jnp.concatenate([high.astype(f32), low.astype(f32)], axis=0)
        turned = pltpu.roll(both, K, 1)
        sources[2 * p] = jnp.where(wide, both, turned)
        sources[2 * p + 1] = jnp.where(wide, turned, both)

    def one(leaf):
        mine = columns[pl.ds(pl.multiple_of(leaf * K, K), K), :]
        own = [jnp.broadcast_to(mine[:, c : c + 1], (K, 2 * K)) for c in range(3)]
        total = jnp.zeros((2 * NV, 2 * K), f32)
        for n in range(0, count, 4):
            highs, lows, lines = [], [], []
            for step in (n, n + 2):
                first = near[leaf * count + step]
                second = near[leaf * count + step + 1]
                place = jnp.where(left, places[first], places[second])
                square = jnp.full((K, 2 * K), soft_square, f32)
                gaps = [own[c] - place[c : c + 1, :] for c in range(3)]
                square = gaps[0] * gaps[0] + gaps[1] * gaps[1] + gaps[2] * gaps[2] + soft_square
                high, low = split(lax.rsqrt(square))
                highs.append(high)
                lows.append(low)
                lines.append(jnp.where(wide, sources[first], sources[second]).astype(bf16))
            kernel = jnp.concatenate(
                [jnp.concatenate(highs, axis=1), jnp.concatenate(lows, axis=1)], axis=0
            )
            total = total + contract(jnp.concatenate(lines, axis=1), kernel, True)
        return (total[:NV, :K] + (total[NV:, :K] + total[:NV, K:])) * scale

    def pair(p, carry):
        out[pl.ds(pl.multiple_of((p - start) * NV, NV), NV), :] = jnp.concatenate(
            [one(2 * p), one(2 * p + 1)], axis=1
        )
        return carry

    lax.fori_loop(start, stop, pair, 0, unroll=4)


def chain_bases(sides, inverse, joined, out):
    inner = [
        mm(joined[j * K : (j + 1) * K, :], two_blocks(inverse[j * K : (j + 1) * K, :]), True)
        for j in range(8)
    ]
    for j in range(8):
        owner = inverse[(j + 1) * K : (j + 2) * K, :]
        mine = chosen(sides[j + 1], owner[:, :K], owner[:, K:]) if j < 7 else owner[:, :K]
        out[j] = mm(mine, inner[j])


def products(
    far_row, far_side, sides, counts, inverse, joined, moment, coupling, chain, pair, couplings, lower_half, upper_half, basis, leaf_q, near0, near1, out, chain_out, coeffs
):
    stacked_rows(lower_half, upper_half, coeffs)
    field = jnp.zeros((NV, K), f32)
    for f in range(2):
        found = inverse[8 * K : 9 * K, K:] if f == 0 else inverse[9 * K : 10 * K, :K]
        high, low = split(mm(moment[:, f * K : (f + 1) * K], found, True))
        field = field + (contract(high, coupling[f], False) + contract(low, coupling[f], False))
    owner = inverse[4 * K : 5 * K, :]
    value = mm(field, chosen(sides[4], owner[:, :K], owner[:, K:]))
    for j in range(3, -1, -1):
        both = mm(value, chain[j * K : (j + 1) * K, :])
        value = chosen(sides[j], both[:, :K], both[:, K:])
    slabs = {1: mm(value, pair[:K, :])}
    for a in range(2, LEAVES, 2):
        both = mm(two_blocks(slabs[a // 2]), pair[(a - 1) * K : (a + 1) * K, :])
        slabs[a] = both[:NV]
        slabs[a + 1] = both[NV:]
    chain_bases(sides, inverse, joined, chain_out)
    lane = lax.broadcasted_iota(jnp.int32, (NV, 2 * K), 1)
    left = lane < K
    for p in range(LEAVES // 2):
        cols = slice(p * 2 * K, (p + 1) * 2 * K)
        lines = []
        for leaf in (2 * p, 2 * p + 1):
            halves = []
            for f in range(4):
                s = leaf * 4 + f
                row = coeffs[pl.ds(pl.multiple_of(far_row[s], NV), NV), :]
                turn = jnp.full((NV, 2 * K), far_side[s], jnp.int32) != (f & 1)
                halves.append(jnp.where(turn, pltpu.roll(row, K, 1), row))
            lines.append(
                jnp.concatenate(
                    [jnp.where(left, halves[0], halves[1]), jnp.where(left, halves[2], halves[3])],
                    axis=1,
                )
            )
        high, low = split(jnp.concatenate(lines, axis=0))
        weights = couplings[:, :, cols].reshape(4 * K, 2 * K)
        part = contract(high, weights, False) + contract(low, weights, False)
        leaf_field = jnp.where(left, part[:NV], part[NV:])
        total = mm(
            jnp.concatenate([slabs[LEAVES // 2 + p], leaf_field], axis=1),
            jnp.concatenate([two_blocks(basis[:, cols]), two_blocks(leaf_q[:, cols])], axis=0),
        )
        live = (lane & K - 1) < jnp.where(left, counts[2 * p], counts[2 * p + 1])
        near = near0 if p < 8 else near1
        out[:, cols] = jnp.where(live, total + near[p % 8 * NV : (p % 8 + 1) * NV, :], 0.0)


def stacked_rows(first, second, out):
    rows = first.shape[0]
    out[:rows, :] = first[...]
    out[rows:, :] = second[...]


def join(first, second, after):
    shape = (2 * first.shape[0], first.shape[1])
    return call(stacked_rows, [(shape, f32)], first, second, after=after)[0]


def turned_ring(x, chips):
    size = lax.axis_size("dev")
    return lax.ppermute(
        x, "dev", [(i, (i + 2 * chips * (1 - 2 * (i & 1))) % size) for i in range(size)]
    )


def moved(x, axis, flip):
    return lax.ppermute(x, axis, [(i, i ^ flip) for i in range(lax.axis_size(axis))])


def per_device(
    points,
    values,
    counts,
    leaf_basis,
    local_pair,
    chain_pair,
    near_leaf,
    far_peer,
    far_leaf,
    leaf_coupling,
    group_far,
    group_coupling,
):
    dev_index = lax.axis_index("dev")
    group_index = lax.axis_index("group")
    pair = local_pair.reshape(31 * K, 2 * K)
    chain = chain_pair.reshape(8 * K, 2 * K)
    bits = jnp.arange(8, dtype=jnp.int32)
    sides = ((group_index * 16 + dev_index) >> bits) & 1
    near_ids = near_leaf.reshape(-1)
    slab = ((K, 2 * K), f32)
    gram, joined, masked, node, share = call(
        upward,
        [
            ((32 * K, 2 * K), f32),
            ((31 * K, 2 * K), f32),
            (values.shape, f32),
            ((40, 2 * K), f32),
            ((40, 2 * K), f32),
        ],
        counts,
        sides,
        leaf_basis,
        values,
        pair,
        chain,
        specs=[SMEM, SMEM] + [pl.BlockSpec(memory_space=pl.ANY)] * 4,
        scratch=[
            pltpu.VMEM(leaf_basis.shape, f32),
            pltpu.VMEM(values.shape, f32),
            pltpu.VMEM((31 * K, 2 * K), f32),
            pltpu.VMEM((K, 2 * K), f32),
            pltpu.SemaphoreType.DMA((4,)),
        ],
        vmem=56,
    )
    double = ((2 * K, 2 * K), f32)
    slabs, joins = [], []

    def climb(level, own, first, second, sends, after):
        axis, base = ("dev", 1 << level) if level < 4 else ("group", 1 << (level - 4))
        near = moved(first, axis, base)
        far = moved(second, axis, 2 * base)
        farther = moved(second, axis, 3 * base)
        body = functools.partial(two_levels, level)
        found = call(
            body,
            [double, double] + [((rows, 2 * K), f32) for rows in sends],
            sides,
            own,
            near,
            far,
            farther,
            chain,
            specs=[SMEM] + [VMEM] * 5,
            after=after,
        )
        slabs.append(found[0])
        joins.append(found[1])
        return found[2:]

    inverse = factor_batch(gram)
    node, share = climb(0, node, node, share, (40, 40), (inverse,))
    leaf_q, coeffs = call(
        bases,
        [(leaf_basis.shape, f32), ((LEAVES // 2 * NV, 2 * K), f32)],
        leaf_basis,
        masked,
        inverse,
        after=(share,),
    )
    (new_pairs,) = call(
        transfers, [((31 * K, 2 * K), f32)], inverse, joined, after=(coeffs,)
    )
    node, share = climb(2, node, node, share, (40, 72), (new_pairs,))
    coeffs = join(coeffs, turned_ring(coeffs, 2), (share,))

    def near_part(start, stop, after):
        return call(
            functools.partial(near_fields, start, stop),
            [(((stop - start) * NV, 2 * K), f32)],
            near_ids,
            points,
            masked,
            specs=[SMEM, VMEM, VMEM],
            scratch=[
                pltpu.VMEM((LEAVES, 8, 2 * K), f32),
                pltpu.VMEM((LEAVES * K, 8), f32),
                pltpu.VMEM((LEAVES, 2 * NV, 2 * K), f32),
            ],
            after=after,
        )[0]

    near0 = near_part(0, 8, (share,))
    send_near, send_far = climb(4, node, node, share, (192, 192), (near0,))
    coeffs = join(coeffs, turned_ring(coeffs, 4), (send_far,))
    near1 = near_part(8, 16, (send_far,))
    near = moved(send_near, "group", 4)
    far = moved(send_far, "group", 8)
    farther = moved(send_far, "group", 12)
    places = ((group_index + 1 + group_far[0]) % 16 ^ group_index).astype(jnp.int32)
    chain_gram, chain_joined, moment = call(
        last_levels,
        [((16 * K, 2 * K), f32), ((8 * K, 2 * K), f32), ((NV, 2 * K), f32)],
        sides,
        places,
        send_near,
        near,
        far,
        farther,
        chain,
        *slabs,
        *joins,
        specs=[SMEM] * 2 + [VMEM] * 11,
        scratch=[
            pltpu.VMEM((640, 2 * K), f32),
            pltpu.VMEM((2 * K, 2 * K), f32),
            pltpu.VMEM((2 * K, 2 * K), f32),
            pltpu.VMEM((40, 2 * K), f32),
        ],
        after=(near1,),
    )
    coeffs = join(coeffs, turned_ring(coeffs, 1), (moment,))
    chain_inverse = factor_batch(chain_gram, 6.5)
    others = moved(coeffs, "dev", 1)
    peer = (dev_index + far_peer) % 16
    core = peer & 1
    apart = (peer >> 1) - (dev_index >> 1)
    hops = jnp.where(core == 0, -apart, apart) & 7
    block = hops >> 1 | (hops & 1) << 2 | (core ^ (dev_index & 1)) << 3
    source = block * (LEAVES // 2 * NV) + (far_leaf >> 1) * NV
    product, chain_out = call(
        products,
        [(values.shape, f32), ((8, K, 2 * K), f32)],
        source.reshape(-1),
        (far_leaf & 1).reshape(-1),
        sides,
        counts,
        chain_inverse,
        chain_joined,
        moment,
        group_coupling,
        chain,
        pair,
        leaf_coupling,
        coeffs,
        others,
        leaf_basis,
        leaf_q,
        near0,
        near1,
        specs=[SMEM] * 4 + [VMEM] * 13,
        us=8.0,
        scratch=[pltpu.VMEM((16 * LEAVES // 2 * NV, 2 * K), f32)],
    )
    chain_out = chain_out.reshape(1, 8, K, 2 * K)
    return (leaf_q, new_pairs.reshape(31, K, 2 * K), chain_out, product)


def solution(mesh):
    both = ("group", "dev")
    in_specs = (
        P(None, both),
        P(None, both),
        P(both),
        P(None, both),
        P(both, None, None),
        P(both, None, None, None),
        P(both, None),
        P(both, None),
        P(both, None),
        P(None, None, both),
        P("group", None),
        P(None, None, "group"),
    )
    out_specs = (
        P(None, both),
        P(both, None, None),
        P(both, None, None, None),
        P(None, both),
    )
    return jax.shard_map(
        per_device, mesh=mesh, in_specs=in_specs, out_specs=out_specs, check_vma=False
    )
```

time: 156 us -> 92 us (0.59)
  Pallas kernels: 73.8 us -> 50 us
  local copies, waits for them, and re-layouts: 21.6 us -> 6.09 us
  between operations: 14.4 us -> 0.93 us
  other arithmetic: 6.44 us -> 0.57 us
  waiting for transfers between devices: 12.1 us -> 6.39 us
    pallas_call x17 -> x15, Pallas kernels: 73.8 us -> 50 us  [call(): pl.pallas_call(kernel, out_shape=[jax.ShapeDtypeStruct(s, d) for s, d in...]
    unnamed x71 -> x41, local copies, waits for them, and re-layouts: 16.9 us -> 5.61 us
    ppermute x8 -> x16, starting transfers between devices: 18.9 us -> 26.8 us  [the longest x13 18.5 us: moved(): lax.ppermute(x, axis, [(i, i ^ flip) for i in range(lax.axis_size(axis))])]
    all_to_all x1 -> x0, starting transfers between devices: 7.33 us -> none  [per_device(): lax.all_to_all(jnp.broadcast_to(root[None], (16, 8, 2 * K)), 'group', 0,...]
    ppermute x8 -> x16, waiting for transfers between devices: 12 us -> 6.39 us  [the longest x3 4.26 us: turned_ring(): lax.ppermute(x, 'dev', [(i, (i + 2 * chips * (1 - 2 * (i & 1))) % size) f...]
    unnamed x7 -> x0, other arithmetic: 3.89 us -> none
    concatenate x9 -> x0, other arithmetic: 1.94 us -> none  [the longest x8 1.86 us: unpacked(): return jnp.concatenate([payload[:half, :K], payload[:half, K:]], axis=0)]
  transfers between devices with their start and end apart: 10 -> 16, of which waited for: 6 -> 4; matrix products, arithmetic and copies ran while one was open for 10% -> 1% of each run, Pallas kernels for 39% -> 34%
where the time goes in v2:
time: 92 us; the launch traced here: 90.8 us
  Pallas kernels  50 us (54%)
  starting transfers between devices  26.8 us (29%)
  waiting for transfers between devices  6.39 us (7%)
  local copies, waits for them, and re-layouts  6.09 us (7%)
  between operations  0.93 us (1%)
    pallas_call x15, Pallas kernels, call(): pl.pallas_call(kernel, out_shape=[jax.ShapeDtypeStruct(s, d) for s, d in...  50 us
    ppermute x13, starting transfers between devices, moved(): lax.ppermute(x, axis, [(i, i ^ flip) for i in range(lax.axis_size(axis))])  18.5 us
    ppermute x3, starting transfers between devices, turned_ring(): lax.ppermute(x, 'dev', [(i, (i + 2 * chips * (1 - 2 * (i & 1))) % size) f...  8.25 us
    unnamed x41, local copies, waits for them, and re-layouts  5.61 us
    ppermute x3, waiting for transfers between devices, turned_ring(): lax.ppermute(x, 'dev', [(i, (i + 2 * chips * (1 - 2 * (i & 1))) % size) f...  4.26 us
    ppermute x13, waiting for transfers between devices, moved(): lax.ppermute(x, axis, [(i, i ^ flip) for i in range(lax.axis_size(axis))])  2.13 us
  transfers between devices with their start and end apart: 16, of which 4 were waited for; matrix products, arithmetic and copies ran while one was open for 1% of the time, Pallas kernels for 34%

profile of v2, /device:TPU:4, one launch (start us, length us, event | category | flops | bytes accessed | tf_op | source)
XLA Modules:
  0.0 90.8 jit_solution(14059213872194462572)
XLA Ops:
  0.6 0.5 shift-right-arithmetic_and_fusion.refs_1_.refs_0_.refs_2_
  1.2 6.8 %upward.1 = (f32[2048,128]{1,0:T(8,128)}, f32[1984,128]{1,0:T(8,128)}, f32[16,2048]{1,0:T(8,128)}, f32[40,128]{1,0:T(8,128)}, f32[40,128]{1,0:T(8,128)}) custom-call(s32[32]{0:T(128)} %refs_3_.3, s32[8]{0:T(128)} %shift-right-arithmetic_and_fusion.refs_1_.refs_0_.refs_2_, f32[64,2048]{1,0:T(8,128)} %refs_13_.1, f32[16,2048]{1,0:T(8,128)} %refs_3_.2, ...), custom_call_target="tpu_custom_call" | custom-call | flops 20000000 | bytes 262144 | tf_op jit(solution)/shard_map/upward/pallas_call | solution.py:66
  8.0 0.1 collective-permute-start
  8.1 2.1 %collective-permute-start.2 = (f32[40,128]{1,0:T(8,128)}, f32[40,128]{1,0:T(8,128)S(1)}, u32[]{:S(2)}, u32[]{:S(2)}) collective-permute-start(f32[40,128]{1,0:T(8,128)} %get-tuple-element.31), channel_id=1, source_target_pairs={{0,3},{1,2},{2,1},{3,0},{4,7},{5,6},{6,5},{7,4},{8,11},{9,10},{10,... | collective-permute-start | bytes 61448 | tf_op jit(solution)/shard_map/ppermute | solution.py:447
  10.2 0.2 collective-permute-start.1
  10.4 1.2 %copy-done.4 = f32[2048,128]{1,0:T(8,128)S(1)} copy-done((f32[2048,128]{1,0:T(8,128)S(1)}, f32[2048,128]{1,0:T(8,128)}, u32[]{:S(2)}) %copy-start.4) | copy-done | bytes 1048600
  11.6 6.8 %inverse_factors.2.refs_6_.refs_2_.refs_0_ = f32[2048,128]{1,0:T(8,128)S(1)} custom-call(f32[2048,128]{1,0:T(8,128)S(1)} %copy-done.4), custom_call_target="tpu_custom_call" | custom-call | flops 20000000 | bytes 262144 | tf_op jit(solution)/shard_map/inverse_factors/pallas_call | solution.py:66
  18.5 0.0 copy-start.2
  18.5 0.0 copy-start.3
  18.5 0.0 collective-permute-done.refs_2_
  18.5 0.0 collective-permute-done.2.refs_4_
  18.5 0.0 collective-permute-done.1.refs_3_
  18.5 1.9 %two_levels.3 = (f32[128,128]{1,0:T(8,128)S(1)}, f32[128,128]{1,0:T(8,128)S(1)}, f32[40,128]{1,0:T(8,128)S(1)}, f32[40,128]{1,0:T(8,128)S(1)}) custom-call(s32[8]{0:T(128)S(1)} %copy-done.9, f32[40,128]{1,0:T(8,128)S(1)} %copy-done.8, f32[40,128]{1,0:T(8,128)S(1)} %collective-permute-done.refs_2_, f32[40,128]{1,0:T(8,128)S(1)} %collective-permute-done.1.refs_3_, ...), custom_call_target="tpu_custom_call" | custom-call | flops 20000000 | bytes 262144 | tf_op jit(solution)/shard_map/two_levels/pallas_call | solution.py:66
  20.5 0.0 copy-done.2
  20.5 2.9 %bases.1 = (f32[64,2048]{1,0:T(8,128)}, f32[256,128]{1,0:T(8,128)S(1)}) custom-call(f32[64,2048]{1,0:T(8,128)S(1)} %copy-done.2, f32[16,2048]{1,0:T(8,128)S(1)} %copy-done.3, f32[2048,128]{1,0:T(8,128)S(1)} %inverse_factors.2.refs_6_.refs_2_.refs_0_, f32[40,128]{1,0:T(8,128)S(1)} %get-tuple-element.32.refs_3_), custom_call_target="tpu_custom_call" | custom-call | flops 20000000 | bytes 262144 | tf_op jit(solution)/shard_map/bases/pallas_call | solution.py:66
  23.4 3.3 %collective-permute-start.12 = (f32[256,128]{1,0:T(8,128)S(1)}, f32[256,128]{1,0:T(8,128)S(1)}, u32[]{:S(2)}, u32[]{:S(2)}) collective-permute-start(f32[256,128]{1,0:T(8,128)S(1)} %get-tuple-element.35.refs_2_.refs_0_), channel_id=1, source_target_pairs={{0,4},{1,13},{2,6},{3,15},{4,8},{5,1},{6,10},{7,3},{8,12},{9,5},{1... | collective-permute-start | bytes 393224 | tf_op jit(solution)/shard_map/ppermute | solution.py:441
  26.6 4.4 %collective-permute-start.3 = (f32[40,128]{1,0:T(8,128)S(1)}, f32[40,128]{1,0:T(8,128)S(1)}, u32[]{:S(2)}, u32[]{:S(2)}) collective-permute-start(f32[40,128]{1,0:T(8,128)S(1)} %get-tuple-element.36.refs_1_), channel_id=1, source_target_pairs={{0,4},{1,5},{2,6},{3,7},{4,0},{5,1},{6,2},{7,3},{8,12},{9,13},{10,... | collective-permute-start | bytes 61448 | tf_op jit(solution)/shard_map/ppermute | solution.py:447
  31.0 1.5 %collective-permute-start.5 = (f32[40,128]{1,0:T(8,128)S(1)}, f32[40,128]{1,0:T(8,128)S(1)}, u32[]{:S(2)}, u32[]{:S(2)}) collective-permute-start(f32[40,128]{1,0:T(8,128)S(1)} %get-tuple-element.32.refs_3_), channel_id=1, source_target_pairs={{0,12},{1,13},{2,14},{3,15},{4,8},{5,9},{6,10},{7,11},{8,4},{9,5},... | collective-permute-start | bytes 61448 | tf_op jit(solution)/shard_map/ppermute | solution.py:447
  32.5 2.1 %collective-permute-start.4 = (f32[40,128]{1,0:T(8,128)S(1)}, f32[40,128]{1,0:T(8,128)S(1)}, u32[]{:S(2)}, u32[]{:S(2)}) collective-permute-start(f32[40,128]{1,0:T(8,128)S(1)} %get-tuple-element.32.refs_3_), channel_id=1, source_target_pairs={{0,8},{1,9},{2,10},{3,11},{4,12},{5,13},{6,14},{7,15},{8,0},{9,1},... | collective-permute-start | bytes 61448 | tf_op jit(solution)/shard_map/ppermute | solution.py:447
  34.6 5.3 %transfers.1.refs_6_ = f32[1984,128]{1,0:T(8,128)} custom-call(f32[2048,128]{1,0:T(8,128)S(1)} %inverse_factors.2.refs_6_.refs_2_.refs_0_, f32[1984,128]{1,0:T(8,128)S(1)} %copy-done.6, f32[256,128]{1,0:T(8,128)S(1)} %get-tuple-element.35.refs_2_.refs_0_), custom_call_target="tpu_custom_call" | custom-call | flops 20000000 | bytes 262144 | tf_op jit(solution)/shard_map/transfers/pallas_call | solution.py:66
  39.9 0.0 collective-permute-done.3.refs_2_
  39.9 0.0 collective-permute-done.5.refs_4_
  39.9 0.3 collective-permute-done.4.refs_3_
  40.2 1.2 %copy-done.1 = f32[1984,128]{1,0:T(8,128)S(1)} copy-done((f32[1984,128]{1,0:T(8,128)S(1)}, f32[1984,128]{1,0:T(8,128)}, u32[]{:S(2)}) %copy-start.1) | copy-done | bytes 1015832
  41.4 1.9 %two_levels.4 = (f32[128,128]{1,0:T(8,128)S(1)}, f32[128,128]{1,0:T(8,128)S(1)}, f32[40,128]{1,0:T(8,128)S(1)}, f32[72,128]{1,0:T(8,128)S(1)}) custom-call(s32[8]{0:T(128)S(1)} %copy-done.9, f32[40,128]{1,0:T(8,128)S(1)} %get-tuple-element.36.refs_1_, f32[40,128]{1,0:T(8,128)S(1)} %collective-permute-done.3.refs_2_, ...), custom_call_target="tpu_custom_call" | custom-call | flops 20000000 | bytes 262144 | tf_op jit(solution)/shard_map/two_levels/pallas_call | solution.py:66
  43.3 0.0 copy-start.16
  43.3 0.0 copy-start.7
  43.3 3.6 %collective-permute-start.13 = (f32[512,128]{1,0:T(8,128)S(1)}, f32[512,128]{1,0:T(8,128)S(1)}, u32[]{:S(2)}, u32[]{:S(2)}) collective-permute-start(f32[512,128]{1,0:T(8,128)S(1)} %stacked_rows.3.refs_0_), channel_id=1, source_target_pairs={{0,8},{1,9},{2,10},{3,11},{4,12},{5,13},{6,14},{7,15},{8,0},{9,1},... | collective-permute-start | bytes 786440 | tf_op jit(solution)/shard_map/ppermute | solution.py:441
  47.0 0.5 collective-permute-start.8
  47.5 2.7 %collective-permute-start.7 = (f32[72,128]{1,0:T(8,128)S(1)}, f32[72,128]{1,0:T(8,128)S(1)}, u32[]{:S(2)}, u32[]{:S(2)}) collective-permute-start(f32[72,128]{1,0:T(8,128)S(1)} %get-tuple-element.38.refs_3_.refs_2_), channel_id=1, source_target_pairs={{0,32},{16,48},{32,0},{48,16},{64,96},{80,112},{96,64},{112,80},{1... | collective-permute-start | bytes 110600 | tf_op jit(solution)/shard_map/ppermute | solution.py:447
  50.3 0.8 collective-permute-start.6
  51.1 0.1 copy.20
  51.2 0.1 reshape.36.refs_0_
  51.3 3.2 %near_fields.2.refs_6_.refs_15_ = f32[128,128]{1,0:T(8,128)S(1)} custom-call(s32[384]{0:T(512)S(1)} %reshape.36.refs_0_, f32[3,2048]{1,0:T(4,128)S(1)} %copy-done.7, f32[16,2048]{1,0:T(8,128)S(1)} %copy-done.3, f32[72,128]{1,0:T(8,128)S(1)} %get-tuple-element.38.refs_3_.refs_2_), custom_call_target="tpu_custom_call" | custom-call | flops 20000000 | bytes 262144 | tf_op jit(solution)/shard_map/near_fields/pallas_call | solution.py:66
  54.5 0.0 collective-permute-done.6.refs_2_
  54.5 0.0 collective-permute-done.8.refs_4_
  54.5 0.0 collective-permute-done.7.refs_3_
  54.5 1.9 %two_levels.5 = (f32[128,128]{1,0:T(8,128)S(1)}, f32[128,128]{1,0:T(8,128)S(1)}, f32[192,128]{1,0:T(8,128)S(1)}, f32[192,128]{1,0:T(8,128)S(1)}) custom-call(s32[8]{0:T(128)S(1)} %copy-done.9, f32[40,128]{1,0:T(8,128)S(1)} %get-tuple-element.37.refs_1_, f32[40,128]{1,0:T(8,128)S(1)} %collective-permute-done.6.refs_2_, ...), custom_call_target="tpu_custom_call" | custom-call | flops 20000000 | bytes 262144 | tf_op jit(solution)/shard_map/two_levels/pallas_call | solution.py:66
  56.4 4.3 %collective-permute-done.13.refs_1_ = f32[512,128]{1,0:T(8,128)S(1)} collective-permute-done((f32[512,128]{1,0:T(8,128)S(1)}, f32[512,128]{1,0:T(8,128)S(1)}, u32[]{:S(2)}, u32[]{:S(2)}) %collective-permute-start.13) | collective-permute-done | bytes 262176 | tf_op jit(solution)/shard_map/ppermute | solution.py:441
  60.7 1.3 %collective-permute-start.14 = (f32[1024,128]{1,0:T(8,128)S(1)}, f32[1024,128]{1,0:T(8,128)S(1)}, u32[]{:S(2)}, u32[]{:S(2)}) collective-permute-start(f32[1024,128]{1,0:T(8,128)S(1)} %stacked_rows.4.refs_0_), channel_id=1, source_target_pairs={{0,2},{1,15},{2,4},{3,1},{4,6},{5,3},{6,8},{7,5},{8,10},{9,7},{10,... | collective-permute-start | bytes 1572872 | tf_op jit(solution)/shard_map/ppermute | solution.py:441
  62.1 3.0 %collective-permute-start.11 = (f32[192,128]{1,0:T(8,128)S(1)}, f32[192,128]{1,0:T(8,128)S(1)}, u32[]{:S(2)}, u32[]{:S(2)}) collective-permute-start(f32[192,128]{1,0:T(8,128)S(1)} %get-tuple-element.40.refs_3_.refs_2_), channel_id=1, source_target_pairs={{0,192},{16,208},{32,224},{48,240},{64,128},{80,144},{96,160},{112... | collective-permute-start | bytes 294920 | tf_op jit(solution)/shard_map/ppermute | solution.py:447
  65.1 0.6 collective-permute-start.10
  65.7 0.5 collective-permute-start.9
  66.2 3.2 %near_fields.3.refs_13_.refs_16_ = f32[128,128]{1,0:T(8,128)S(1)} custom-call(s32[384]{0:T(512)S(1)} %reshape.36.refs_0_, f32[3,2048]{1,0:T(4,128)S(1)} %copy-done.7, f32[16,2048]{1,0:T(8,128)S(1)} %copy-done.3, f32[192,128]{1,0:T(8,128)S(1)} %get-tuple-element.40.refs_3_.refs_2_), custom_call_target="tpu_custom_call" | custom-call | flops 20000000 | bytes 262144 | tf_op jit(solution)/shard_map/near_fields/pallas_call | solution.py:66
  69.3 1.0 %collective-permute-done.9.refs_3_ = f32[192,128]{1,0:T(8,128)S(1)} collective-permute-done((f32[192,128]{1,0:T(8,128)S(1)}, f32[192,128]{1,0:T(8,128)S(1)}, u32[]{:S(2)}, u32[]{:S(2)}) %collective-permute-start.9) | collective-permute-done | bytes 98336 | tf_op jit(solution)/shard_map/ppermute | solution.py:447
  70.3 0.0 collective-permute-done.11.refs_5_
  70.3 0.9 collective-permute-done.10.refs_4_
  71.2 1.6 %last_levels.1 = (f32[1024,128]{1,0:T(8,128)S(1)}, f32[512,128]{1,0:T(8,128)S(1)}, f32[16,128]{1,0:T(8,128)S(1)}) custom-call(s32[8]{0:T(128)S(1)} %copy-done.9, s32[2]{0:T(128)S(1)} %fusion.2.refs_1_, f32[192,128]{1,0:T(8,128)S(1)} %get-tuple-element.39.refs_2_, f32[192,128]{1,0:T(8,128)S(1)} %collective-permute-done.9.refs_3_, ...), custom_call_target="tpu_custom_call" | custom-call | flops 20000000 | bytes 262144 | tf_op jit(solution)/shard_map/last_levels/pallas_call | solution.py:66
  72.8 0.0 collective-permute-done.14.refs_1_
  72.8 0.0 copy-start.18
  72.8 0.1 stacked_rows.5.refs_11_
  72.9 0.7 copy-done.13
  73.6 0.0 collective-permute-start.15
  73.6 0.7 copy-done.17
  74.3 0.1 copy.19
  74.3 0.1 reshape.35.refs_1_
  74.4 0.1 copy.18
  74.5 0.1 reshape.34.refs_0_
  74.7 1.0 %copy-done.14 = f32[1024,128]{1,0:T(8,128)S(1)} copy-done((f32[1024,128]{1,0:T(8,128)S(1)}, f32[1024,128]{1,0:T(8,128)}, u32[]{:S(2)}) %copy-start.14) | copy-done | bytes 524312
  75.7 6.5 %inverse_factors.3.refs_4_ = f32[1024,128]{1,0:T(8,128)S(1)} custom-call(f32[1024,128]{1,0:T(8,128)S(1)} %copy-done.14), custom_call_target="tpu_custom_call" | custom-call | flops 6499999744 | bytes 262144 | tf_op jit(solution)/shard_map/inverse_factors/pallas_call | solution.py:66
  82.2 0.0 collective-permute-done.15.refs_12_
  82.3 0.0 copy-start.10
  82.3 0.6 copy-done.10
  82.9 7.9 %products.1 = (f32[16,2048]{1,0:T(8,128)}, f32[8,64,128]{2,1,0:T(8,128)}) custom-call(s32[128]{0:T(128)S(1)} %reshape.34.refs_0_, s32[128]{0:T(128)S(1)} %reshape.35.refs_1_, s32[8]{0:T(128)S(1)} %copy-done.9, s32[32]{0:T(128)S(1)} %copy-done.10, f32[1024,128]{1,0:T(8,128)S(1)} %inverse_factors.3.refs_4_, f32[512,128]{1,0:T(8,128)S(1)} %get-tuple-element.48.refs_5_, ...), custom_call_target="tpu_custom_call" | custom-call | flops 8000000000 | bytes 262144 | tf_op jit(solution)/shard_map/products/pallas_call | solution.py:66
  (32 shorter events, 0.1 us)
Async XLA Ops:
  8.0 10.5 %collective-permute-start = (f32[40,128]{1,0:T(8,128)}, f32[40,128]{1,0:T(8,128)S(1)}, u32[]{:S(2)}, u32[]{:S(2)}) collective-permute-start(f32[40,128]{1,0:T(8,128)} %get-tuple-element.30.refs_1_), channel_id=1, source_target_pairs={{0,1},{1,0},{2,3},{3,2},{4,5},{5,4},{6,7},{7,6},{8,9},{9,8},{10,11... | collective-permute-start | bytes 61448 | tf_op jit(solution)/shard_map/ppermute | solution.py:447
  8.1 10.4 %collective-permute-start.2 = (f32[40,128]{1,0:T(8,128)}, f32[40,128]{1,0:T(8,128)S(1)}, u32[]{:S(2)}, u32[]{:S(2)}) collective-permute-start(f32[40,128]{1,0:T(8,128)} %get-tuple-element.31), channel_id=1, source_target_pairs={{0,3},{1,2},{2,1},{3,0},{4,7},{5,6},{6,5},{7,4},{8,11},{9,10},{10,... | collective-permute-start | bytes 61448 | tf_op jit(solution)/shard_map/ppermute | solution.py:447
  10.2 8.4 %collective-permute-start.1 = (f32[40,128]{1,0:T(8,128)}, f32[40,128]{1,0:T(8,128)S(1)}, u32[]{:S(2)}, u32[]{:S(2)}) collective-permute-start(f32[40,128]{1,0:T(8,128)} %get-tuple-element.31), channel_id=1, source_target_pairs={{0,2},{1,3},{2,0},{3,1},{4,6},{5,7},{6,4},{7,5},{8,10},{9,11},{10,... | collective-permute-start | bytes 61448 | tf_op jit(solution)/shard_map/ppermute | solution.py:447
  10.4 1.2 %copy-start.4 = (f32[2048,128]{1,0:T(8,128)S(1)}, f32[2048,128]{1,0:T(8,128)}, u32[]{:S(2)}) copy-start(f32[2048,128]{1,0:T(8,128)} %get-tuple-element.29.refs_0_) | copy-start | bytes 3145732
  11.6 6.9 %copy-start = (f32[1,8,64,128]{3,2,1,0:T(8,128)S(1)}, f32[1,8,64,128]{3,2,1,0:T(8,128)}, u32[]{:S(2)}) copy-start(f32[1,8,64,128]{3,2,1,0:T(8,128)} %param.17) | copy-start | bytes 786436
  11.6 6.9 %copy-start.8 = (f32[40,128]{1,0:T(8,128)S(1)}, f32[40,128]{1,0:T(8,128)}, u32[]{:S(2)}) copy-start(f32[40,128]{1,0:T(8,128)} %get-tuple-element.30.refs_1_) | copy-start | bytes 61444
  11.6 6.9 %copy-start.9 = (s32[8]{0:T(128)S(1)}, s32[8]{0:T(128)}, u32[]{:S(2)}) copy-start(s32[8]{0:T(128)} %shift-right-arithmetic_and_fusion.refs_1_.refs_0_.refs_2_) | copy-start | bytes 100
  18.5 2.0 %copy-start.2 = (f32[64,2048]{1,0:T(8,128)S(1)}, f32[64,2048]{1,0:T(8,128)}, u32[]{:S(2)}) copy-start(f32[64,2048]{1,0:T(8,128)} %refs_13_.1) | copy-start | bytes 1572868
  18.5 2.0 %copy-start.3 = (f32[16,2048]{1,0:T(8,128)S(1)}, f32[16,2048]{1,0:T(8,128)}, u32[]{:S(2)}) copy-start(f32[16,2048]{1,0:T(8,128)} %get-tuple-element.28.refs_1_.refs_2_) | copy-start | bytes 393220
  20.5 14.1 %copy-start.6 = (f32[1984,128]{1,0:T(8,128)S(1)}, f32[1984,128]{1,0:T(8,128)}, u32[]{:S(2)}) copy-start(f32[1984,128]{1,0:T(8,128)} %get-tuple-element.34.refs_1_) | copy-start | bytes 3047428
  23.4 19.9 %collective-permute-start.12 = (f32[256,128]{1,0:T(8,128)S(1)}, f32[256,128]{1,0:T(8,128)S(1)}, u32[]{:S(2)}, u32[]{:S(2)}) collective-permute-start(f32[256,128]{1,0:T(8,128)S(1)} %get-tuple-element.35.refs_2_.refs_0_), channel_id=1, source_target_pairs={{0,4},{1,13},{2,6},{3,15},{4,8},{5,1},{6,10},{7,3},{8,12},{9,5},{1... | collective-permute-start | bytes 393224 | tf_op jit(solution)/shard_map/ppermute | solution.py:441
  26.6 13.2 %collective-permute-start.3 = (f32[40,128]{1,0:T(8,128)S(1)}, f32[40,128]{1,0:T(8,128)S(1)}, u32[]{:S(2)}, u32[]{:S(2)}) collective-permute-start(f32[40,128]{1,0:T(8,128)S(1)} %get-tuple-element.36.refs_1_), channel_id=1, source_target_pairs={{0,4},{1,5},{2,6},{3,7},{4,0},{5,1},{6,2},{7,3},{8,12},{9,13},{10,... | collective-permute-start | bytes 61448 | tf_op jit(solution)/shard_map/ppermute | solution.py:447
  31.0 8.9 %collective-permute-start.5 = (f32[40,128]{1,0:T(8,128)S(1)}, f32[40,128]{1,0:T(8,128)S(1)}, u32[]{:S(2)}, u32[]{:S(2)}) collective-permute-start(f32[40,128]{1,0:T(8,128)S(1)} %get-tuple-element.32.refs_3_), channel_id=1, source_target_pairs={{0,12},{1,13},{2,14},{3,15},{4,8},{5,9},{6,10},{7,11},{8,4},{9,5},... | collective-permute-start | bytes 61448 | tf_op jit(solution)/shard_map/ppermute | solution.py:447
  32.5 7.7 %collective-permute-start.4 = (f32[40,128]{1,0:T(8,128)S(1)}, f32[40,128]{1,0:T(8,128)S(1)}, u32[]{:S(2)}, u32[]{:S(2)}) collective-permute-start(f32[40,128]{1,0:T(8,128)S(1)} %get-tuple-element.32.refs_3_), channel_id=1, source_target_pairs={{0,8},{1,9},{2,10},{3,11},{4,12},{5,13},{6,14},{7,15},{8,0},{9,1},... | collective-permute-start | bytes 61448 | tf_op jit(solution)/shard_map/ppermute | solution.py:447
  40.1 1.2 %copy-start.1 = (f32[1984,128]{1,0:T(8,128)S(1)}, f32[1984,128]{1,0:T(8,128)}, u32[]{:S(2)}) copy-start(f32[1984,128]{1,0:T(8,128)} %transfers.1.refs_6_) | copy-start | bytes 3047428
  43.3 7.8 %copy-start.16 = (s32[32,12]{0,1:T(8,128)S(1)}, s32[32,12]{0,1:T(8,128)}, u32[]{:S(2)}) copy-start(s32[32,12]{0,1:T(8,128)} %param.18) | copy-start | bytes 4612
  43.3 7.9 %copy-start.7 = (f32[3,2048]{1,0:T(4,128)S(1)}, f32[3,2048]{1,0:T(4,128)}, u32[]{:S(2)}) copy-start(f32[3,2048]{1,0:T(4,128)} %refs_1_.3) | copy-start | bytes 73732
  43.3 17.3 %collective-permute-start.13 = (f32[512,128]{1,0:T(8,128)S(1)}, f32[512,128]{1,0:T(8,128)S(1)}, u32[]{:S(2)}, u32[]{:S(2)}) collective-permute-start(f32[512,128]{1,0:T(8,128)S(1)} %stacked_rows.3.refs_0_), channel_id=1, source_target_pairs={{0,8},{1,9},{2,10},{3,11},{4,12},{5,13},{6,14},{7,15},{8,0},{9,1},... | collective-permute-start | bytes 786440 | tf_op jit(solution)/shard_map/ppermute | solution.py:441
  47.0 7.5 %collective-permute-start.8 = (f32[72,128]{1,0:T(8,128)S(1)}, f32[72,128]{1,0:T(8,128)S(1)}, u32[]{:S(2)}, u32[]{:S(2)}) collective-permute-start(f32[72,128]{1,0:T(8,128)S(1)} %get-tuple-element.38.refs_3_.refs_2_), channel_id=1, source_target_pairs={{0,48},{16,32},{32,16},{48,0},{64,112},{80,96},{96,80},{112,64},{1... | collective-permute-start | bytes 110600 | tf_op jit(solution)/shard_map/ppermute | solution.py:447
  47.5 6.9 %collective-permute-start.7 = (f32[72,128]{1,0:T(8,128)S(1)}, f32[72,128]{1,0:T(8,128)S(1)}, u32[]{:S(2)}, u32[]{:S(2)}) collective-permute-start(f32[72,128]{1,0:T(8,128)S(1)} %get-tuple-element.38.refs_3_.refs_2_), channel_id=1, source_target_pairs={{0,32},{16,48},{32,0},{48,16},{64,96},{80,112},{96,64},{112,80},{1... | collective-permute-start | bytes 110600 | tf_op jit(solution)/shard_map/ppermute | solution.py:447
  50.3 4.2 %collective-permute-start.6 = (f32[40,128]{1,0:T(8,128)S(1)}, f32[40,128]{1,0:T(8,128)S(1)}, u32[]{:S(2)}, u32[]{:S(2)}) collective-permute-start(f32[40,128]{1,0:T(8,128)S(1)} %get-tuple-element.37.refs_1_), channel_id=1, source_target_pairs={{0,16},{16,0},{32,48},{48,32},{64,80},{80,64},{96,112},{112,96},{1... | collective-permute-start | bytes 61448 | tf_op jit(solution)/shard_map/ppermute | solution.py:447
  60.7 12.1 %collective-permute-start.14 = (f32[1024,128]{1,0:T(8,128)S(1)}, f32[1024,128]{1,0:T(8,128)S(1)}, u32[]{:S(2)}, u32[]{:S(2)}) collective-permute-start(f32[1024,128]{1,0:T(8,128)S(1)} %stacked_rows.4.refs_0_), channel_id=1, source_target_pairs={{0,2},{1,15},{2,4},{3,1},{4,6},{5,3},{6,8},{7,5},{8,10},{9,7},{10,... | collective-permute-start | bytes 1572872 | tf_op jit(solution)/shard_map/ppermute | solution.py:441
  62.1 4.1 %copy-start.19 = (s32[1,2]{1,0:T(1,128)S(1)}, s32[1,2]{1,0:T(1,128)}, u32[]{:S(2)}) copy-start(s32[1,2]{1,0:T(1,128)} %param.22) | copy-start | bytes 28
  62.1 8.3 %collective-permute-start.11 = (f32[192,128]{1,0:T(8,128)S(1)}, f32[192,128]{1,0:T(8,128)S(1)}, u32[]{:S(2)}, u32[]{:S(2)}) collective-permute-start(f32[192,128]{1,0:T(8,128)S(1)} %get-tuple-element.40.refs_3_.refs_2_), channel_id=1, source_target_pairs={{0,192},{16,208},{32,224},{48,240},{64,128},{80,144},{96,160},{112... | collective-permute-start | bytes 294920 | tf_op jit(solution)/shard_map/ppermute | solution.py:447
  65.1 6.1 %collective-permute-start.10 = (f32[192,128]{1,0:T(8,128)S(1)}, f32[192,128]{1,0:T(8,128)S(1)}, u32[]{:S(2)}, u32[]{:S(2)}) collective-permute-start(f32[192,128]{1,0:T(8,128)S(1)} %get-tuple-element.40.refs_3_.refs_2_), channel_id=1, source_target_pairs={{0,128},{16,144},{32,160},{48,176},{64,192},{80,208},{96,224},{112... | collective-permute-start | bytes 294920 | tf_op jit(solution)/shard_map/ppermute | solution.py:447
  65.7 4.6 %collective-permute-start.9 = (f32[192,128]{1,0:T(8,128)S(1)}, f32[192,128]{1,0:T(8,128)S(1)}, u32[]{:S(2)}, u32[]{:S(2)}) collective-permute-start(f32[192,128]{1,0:T(8,128)S(1)} %get-tuple-element.39.refs_2_), channel_id=1, source_target_pairs={{0,64},{16,80},{32,96},{48,112},{64,0},{80,16},{96,32},{112,48},{1... | collective-permute-start | bytes 294920 | tf_op jit(solution)/shard_map/ppermute | solution.py:447
  72.8 0.8 copy-start.13
  72.8 0.8 copy-start.18
  73.5 0.7 copy-start.17
  73.6 8.7 %collective-permute-start.15 = (f32[2048,128]{1,0:T(8,128)S(1)}, f32[2048,128]{1,0:T(8,128)}, u32[]{:S(2)}, u32[]{:S(2)}) collective-permute-start(f32[2048,128]{1,0:T(8,128)S(1)} %stacked_rows.5.refs_11_), channel_id=1, source_target_pairs={{0,1},{1,0},{2,3},{3,2},{4,5},{5,4},{6,7},{7,6},{8,9},{9,8},{10,11... | collective-permute-start | bytes 3145736 | tf_op jit(solution)/shard_map/ppermute | solution.py:447
  74.6 1.0 %copy-start.14 = (f32[1024,128]{1,0:T(8,128)S(1)}, f32[1024,128]{1,0:T(8,128)}, u32[]{:S(2)}) copy-start(f32[1024,128]{1,0:T(8,128)} %copy-done.13) | copy-start | bytes 1572868
  75.7 6.6 %copy-start.5 = (f32[31,64,128]{2,1,0:T(8,128)S(1)}, f32[31,64,128]{2,1,0:T(8,128)}, u32[]{:S(2)}) copy-start(f32[31,64,128]{2,1,0:T(8,128)} %param.16) | copy-start | bytes 3047428
  75.7 6.6 %copy-start.11 = (bf16[4,64,2048]{2,1,0:T(8,128)(2,1)S(1)}, bf16[4,64,2048]{2,1,0:T(8,128)(2,1)}, u32[]{:S(2)}) copy-start(bf16[4,64,2048]{2,1,0:T(8,128)(2,1)} %refs_10_.1) | copy-start | bytes 3145732
  75.7 6.6 %copy-start.12 = (f32[64,2048]{1,0:T(8,128)S(1)}, f32[64,2048]{1,0:T(8,128)}, u32[]{:S(2)}) copy-start(f32[64,2048]{1,0:T(8,128)} %get-tuple-element.24.refs_14_) | copy-start | bytes 1572868
  75.7 6.6 %copy-start.15 = (bf16[2,64,64]{2,1,0:T(8,128)(2,1)S(1)}, bf16[2,64,64]{2,1,0:T(8,128)(2,1)}, u32[]{:S(2)}) copy-start(bf16[2,64,64]{2,1,0:T(8,128)(2,1)} %refs_7_.1) | copy-start | bytes 49156
  82.3 0.7 copy-start.10
